TPU v7x, 32 devices: a whole 2x2x4 slice. The times are simulated.
32 devices in a mesh: wide: 8 (over y, x, core), narrow: 4 (over z).
Axes of the slice: x: 2, y: 2, z: 4, core: 2. Of those that a mesh axis runs over, the one named last changes fastest.
Arguments:
- tokens: bfloat16 [32768, 512], P(('wide', 'narrow')), may hold values from -6 to 6
- segment_ids: int32 [32768], P(('wide', 'narrow')), may hold values from 0 to 20, as said below
- expert_picks: int32 [32768, 2], P(('wide', 'narrow')), may hold values from 0 to 7, all different within a row; in each aligned block of 1024 rows (0 to 1023, 1024 to 2047, ...) at most 271 rows name the same one
- priority_ranks: int32 [32, 1024], P(('wide', 'narrow')), may hold values from 0 to 1023, each once within a row
- gain_attn: float32 [512], replicated, may hold values from 0.1 to 1.9
- w_qkv: bfloat16 [512, 1536], replicated, may hold values from -0.25 to 0.25
- w_proj: bfloat16 [512, 512], replicated, may hold values from -2 to 2
- gain_moe: float32 [512], replicated, may hold values from 0.1 to 1.9
- w_router: bfloat16 [512, 8], replicated, may hold values from -0.25 to 0.25
- w_in: bfloat16 [8, 512, 2048], P('wide', None, 'narrow'), may hold values from -0.25 to 0.25
- w_out: bfloat16 [8, 2048, 512], P('wide', 'narrow'), may hold values from -0.75 to 0.75
- cotangent: bfloat16 [32768, 512], P(('wide', 'narrow')), may hold values from -6 to 6
Outputs:
- mixed: bfloat16 [32768, 512], P(('wide', 'narrow'))
- grad_tokens: float32 [32768, 512], P(('wide', 'narrow'))
- grad_gain_attn: float32 [512], replicated
- grad_qkv: float32 [512, 1536], replicated
- grad_proj: float32 [512, 512], replicated
- grad_gain_moe: float32 [512], replicated
- grad_router: float32 [512, 8], replicated
- grad_in: float32 [8, 512, 2048], P('wide', None, 'narrow')
- grad_out: float32 [8, 2048, 512], P('wide', 'narrow')
- kept_counts: int32 [8], replicated
- dropped_counts: int32 [8], replicated
Inputs may be any that keep to these rules, and one draw needn't show every extreme that they name: `expert_picks`: within each aligned block of 1024 tokens (one routing group) no expert is picked more than 269 + 2 times, and in some block one is picked exactly that often; a token's 2 picks differ; every expert is picked somewhere. `priority_ranks`: each row is a permutation of one routing group's positions; rank 0 comes first. `segment_ids`: each run of 1024 slots is one sequence of whole images of 49 or 144 patches, numbered from 0 up in order; the slots after the last whole image form one more segment. Some sequence holds only images of 49 patches.
All inputs are finite; a program needn't handle non-finite values.
Results may differ from a plain program's by a relative error of at most 0.015.
The roundings to bfloat16 on the way count: a program that leaves them out, or rounds other values in their place, can miss the bound.
Values may be sent and summed in bfloat16 or wider, within the bound.
A program may use at most 256 MiB of HBM per device.

v0:
```python
import functools

import jax
import jax.numpy as jnp
from jax import lax
from jax.experimental import pallas as pl
from jax.experimental.pallas import tpu as pltpu
from jax.sharding import PartitionSpec as P

D = 512
HEADS = 8
HEAD = 64
PAIRS = HEADS // 2
PAIR = 2 * HEAD
TOP = 2
SEQ = 1024
TOK_DEV = 1024
LANES = 128
QB = 128
WINDOW = 432
TILE = 256
MIB = 1024 * 1024
MESH = pl.DeviceIdType.MESH

f32 = jnp.float32
bf16 = jnp.bfloat16
NT = (((1,), (1,)), ((), ()))
TN = (((0,), (0,)), ((), ()))


def dot(a, b):
    return jnp.dot(a, b, preferred_element_type=f32)


def dot_nt(a, b):
    return lax.dot_general(a, b, NT, preferred_element_type=f32)


def dot_tn(a, b):
    return lax.dot_general(a, b, TN, preferred_element_type=f32)


def iota(shape, dim):
    return lax.broadcasted_iota(jnp.int32, shape, dim)


def norm_parts(values_in):
    centered = values_in - jnp.mean(values_in, axis=-1, keepdims=True)
    variance = jnp.mean(centered * centered, axis=-1, keepdims=True)
    inverse = lax.rsqrt(variance + 1e-06)
    return (centered * inverse, inverse)


def norm_back(grad_normed, gain, normalized, inverse):
    grad_gain = jnp.sum(grad_normed * normalized, axis=0, keepdims=True)
    scaled = grad_normed * gain
    inner = scaled - jnp.mean(scaled, axis=-1, keepdims=True)
    inner = inner - normalized * jnp.mean(scaled * normalized, axis=-1, keepdims=True)
    return (inner * inverse, grad_gain)


def split2(values_in):
    high = values_in.astype(bf16)
    low = (values_in - high.astype(f32)).astype(bf16)
    return high, low


def row_to_col(row):
    n = row.shape[1]
    return jnp.transpose(jnp.broadcast_to(row, (LANES, n)))[:, :1]


def route_kernel(experts, capacity, picks, ranks, cot, slot_col, slot_row, counts, gz_send):
    tokens = ranks.shape[1]
    padded = gz_send.shape[1]
    rank_row = ranks[...].astype(f32)
    rank_col = row_to_col(rank_row)
    lane = iota((tokens, LANES), 1)
    pick0 = picks[:, 0:1]
    pick1 = picks[:, 1:2]
    hot = jnp.where(lane == jnp.where(lane < experts, pick0, pick1 + experts), 1.0, 0.0).astype(f32)
    before = (rank_row < rank_col).astype(f32).astype(bf16)
    earlier = dot(before, hot.astype(bf16))
    total = jnp.sum(hot, axis=0, keepdims=True)
    total = jnp.broadcast_to(total, (8, LANES))
    lane8 = iota((8, LANES), 1)
    first = jnp.where(lane8 < experts, total, 0.0)
    earlier = earlier + pltpu.roll(first, experts, axis=1)[:1]
    kept = (hot > 0.5) & (earlier < float(capacity))
    slots = jnp.where(kept, earlier, -1.0)
    slot_col[...] = slots
    slots = jnp.maximum(slots, pltpu.roll(slots, LANES - experts, axis=1))
    slots = jnp.where(lane < experts, slots, -1.0)
    slot_row[...] = jnp.transpose(slots)[:experts]
    kept_lane = jnp.sum(jnp.where(slots >= 0.0, 1.0, 0.0), axis=0, keepdims=True)
    both = total + pltpu.roll(total, LANES - experts, axis=1)
    both = jnp.where(lane8 < experts, both, 0.0)
    sub8 = iota((8, LANES), 0)
    counts[...] = jnp.where(sub8 == 0, kept_lane, jnp.where(sub8 == 1, both, 0.0))

    @pl.loop(0, experts)
    def _(e):
        chosen = iota((padded, tokens), 0).astype(f32) == slot_row[pl.ds(e, 1), :]
        gz_send[e] = dot(chosen.astype(f32).astype(bf16), cot[...]).astype(bf16)


def route(picks, ranks, cot, experts, capacity, padded):
    tokens = picks.shape[0]
    return pl.pallas_call(
        functools.partial(route_kernel, experts, capacity),
        out_shape=(
            jax.ShapeDtypeStruct((tokens, LANES), f32),
            jax.ShapeDtypeStruct((experts, tokens), f32),
            jax.ShapeDtypeStruct((8, LANES), f32),
            jax.ShapeDtypeStruct((experts, padded, D), bf16),
        ),
        compiler_params=pltpu.CompilerParams(vmem_limit_bytes=40 * MIB),
        cost_estimate=pl.CostEstimate(
            flops=2 * experts * padded * tokens * D, bytes_accessed=6 * MIB, transcendentals=0
        ),
        name="route",
    )(picks, ranks, cot)


def stack_heads(block):
    lane = iota(block.shape, 1)
    zero = jnp.zeros_like(block)
    return jnp.concatenate(
        [jnp.where(lane < HEAD, block, zero), jnp.where(lane < HEAD, zero, block)], axis=0
    )


def unstack_cols(stacked):
    row = iota((PAIR, QB), 0)
    picked = jnp.where(row < HEAD, stacked[:, :QB], stacked[:, QB:])
    return jnp.transpose(picked)


def window_bias(seg_col, seg_row, low, width, query):
    same = seg_col[pl.ds(low, width), :] == seg_row[:, pl.ds(query, QB)]
    half = jnp.where(same, 0.0, -1e30).astype(f32)
    return jnp.concatenate([half, half], axis=1)


def by_window(windows, block, body):
    low = windows[block]
    fits = windows[block + SEQ // QB]

    @pl.when(fits == 1)
    def _():
        body(pl.multiple_of(low, 16), WINDOW)

    @pl.when(fits != 1)
    def _():
        body(0, SEQ)


def forward_kernel(
    experts,
    windows,
    tok,
    seg,
    gain_attn,
    w_qkv,
    w_proj,
    gain_moe,
    w_router,
    normed_attn_out,
    packed_out,
    context_out,
    lse,
    residual_out,
    normed_moe_out,
    gates_out,
    gate_row,
    normed_attn,
    packed,
    context,
    residual,
    normed_moe,
    gates,
    seg_col,
    seg_row,
    router,
    sems,
):
    writes = [
        pltpu.make_async_copy(source, target, sems.at[i])
        for i, (source, target) in enumerate(
            (
                (normed_attn, normed_attn_out),
                (packed, packed_out),
                (context, context_out),
                (residual, residual_out),
                (normed_moe, normed_moe_out),
                (gates, gates_out),
            )
        )
    ]
    tokens = tok.shape[0]
    seg_row[...] = seg[...].astype(f32)
    seg_col[...] = jnp.transpose(jnp.broadcast_to(seg_row[...], (LANES, tokens)))
    router[...] = jnp.zeros_like(router)
    router[:, :experts] = w_router[...]

    @pl.loop(0, tokens // TILE)
    def _(i):
        rows = pl.ds(pl.multiple_of(i * TILE, TILE), TILE)
        normal, unused = norm_parts(tok[rows, :].astype(f32))
        normed = (normal * gain_attn[...]).astype(bf16)
        normed_attn[rows, :] = normed
        packed[rows, :] = dot(normed, w_qkv[...]).astype(bf16)

    writes[0].start()
    writes[1].start()

    @pl.loop(0, tokens // QB)
    def _(block):
        query = pl.multiple_of(block * QB, QB)

        def body(low, width):
            bias = window_bias(seg_col, seg_row, low, width, query)
            spans = [slice(pair * PAIR, (pair + 1) * PAIR) for pair in range(PAIRS)]
            scores = []
            for span in spans:
                q = stack_heads(packed[pl.ds(query, QB), span]) * HEAD ** (-0.5)
                k = packed[pl.ds(low, width), D + span.start : D + span.stop]
                scores.append(dot_nt(k, q.astype(bf16)) + bias)
            peaks = [jnp.max(score, axis=0, keepdims=True) for score in scores]
            exponents = [jnp.exp(score - peak) for score, peak in zip(scores, peaks)]
            totals = [jnp.sum(exponent, axis=0, keepdims=True) for exponent in exponents]
            probs = [(exponent * (1.0 / total)).astype(bf16) for exponent, total in zip(exponents, totals)]
            for pair, span in enumerate(spans):
                lse[pl.ds(block, 1), pair, :] = peaks[pair] + jnp.log(totals[pair])
                v = packed[pl.ds(low, width), 2 * D + span.start : 2 * D + span.stop]
                mixed = dot_tn(v, probs[pair])
                context[pl.ds(query, QB), span] = unstack_cols(mixed).astype(bf16)

        by_window(windows, block, body)

    writes[2].start()

    @pl.loop(0, tokens // TILE)
    def _(i):
        rows = pl.ds(pl.multiple_of(i * TILE, TILE), TILE)
        rest = tok[rows, :].astype(f32) + dot(context[rows, :], w_proj[...])
        residual[rows, :] = rest
        normal, unused = norm_parts(rest)
        normed = (normal * gain_moe[...]).astype(bf16)
        normed_moe[rows, :] = normed
        logits = dot(normed, router[...])
        logits = jnp.where(iota(logits.shape, 1) < experts, logits, -1e30)
        exponent = jnp.exp(logits - jnp.max(logits, axis=1, keepdims=True))
        gates[rows, :] = exponent / jnp.sum(exponent, axis=1, keepdims=True)

    for write in writes[3:]:
        write.start()
    gate_row[...] = jnp.transpose(gates[...])[:experts]
    for write in writes:
        write.wait()


def forward(windows, tok, seg, gain_attn, w_qkv, w_proj, gain_moe, w_router):
    tokens = tok.shape[0]
    experts = w_router.shape[1]
    vmem = pl.BlockSpec(memory_space=pltpu.VMEM)
    anywhere = pl.BlockSpec(memory_space=pl.ANY)
    return pl.pallas_call(
        functools.partial(forward_kernel, experts),
        in_specs=[pl.BlockSpec(memory_space=pltpu.SMEM)] + [vmem] * 7,
        out_specs=[anywhere] * 3 + [vmem] + [anywhere] * 3 + [vmem],
        out_shape=(
            jax.ShapeDtypeStruct((tokens, D), bf16),
            jax.ShapeDtypeStruct((tokens, 3 * D), bf16),
            jax.ShapeDtypeStruct((tokens, D), bf16),
            jax.ShapeDtypeStruct((tokens // QB, PAIRS, 2 * QB), f32),
            jax.ShapeDtypeStruct((tokens, D), f32),
            jax.ShapeDtypeStruct((tokens, D), bf16),
            jax.ShapeDtypeStruct((tokens, LANES), f32),
            jax.ShapeDtypeStruct((experts, tokens), f32),
        ),
        scratch_shapes=[
            pltpu.VMEM((tokens, D), bf16),
            pltpu.VMEM((tokens, 3 * D), bf16),
            pltpu.VMEM((tokens, D), bf16),
            pltpu.VMEM((tokens, D), f32),
            pltpu.VMEM((tokens, D), bf16),
            pltpu.VMEM((tokens, LANES), f32),
            pltpu.VMEM((tokens, LANES), f32),
            pltpu.VMEM((1, tokens), f32),
            pltpu.VMEM((D, LANES), bf16),
            pltpu.SemaphoreType.DMA((6,)),
        ],
        compiler_params=pltpu.CompilerParams(vmem_limit_bytes=56 * MIB),
        cost_estimate=pl.CostEstimate(
            flops=8 * 1024 * MIB, bytes_accessed=16 * MIB, transcendentals=4 * MIB
        ),
        name="attention_forward",
    )(windows, tok, seg, gain_attn, w_qkv, w_proj, gain_moe, w_router)


def gelu_parts(x):
    density = jnp.exp(-0.5 * (x * x))
    return 0.5 + 0.5 * lax.erf(x * 2.0**-0.5), x * density * 0.3989422804014327


def shifted(index, by, size):
    return lax.rem(index + by, size)


def paired(index, by, size):
    total = 0
    bit = 1
    while bit < size:
        total = total + bit * lax.rem(index // bit + by // bit, 2)
        bit *= 2
    return total


def exchange(src, dst, send, recv, device):
    return pltpu.make_async_remote_copy(
        src_ref=src, dst_ref=dst, send_sem=send, recv_sem=recv, device_id=device, device_id_type=MESH
    )


def greet(barrier, sources):
    me = lax.axis_index("wide")
    line = lax.axis_index("narrow")

    @pl.loop(1, sources)
    def _(j):
        pl.semaphore_signal(barrier, inc=1, device_id=(paired(me, j, sources), line), device_id_type=MESH)


def dispatch_kernel(
    shards, slot_row, gate_row, normed_moe, first, received, weights, rows_send, gate_slot, send, recv, own_sem, ring_sem
):
    experts, padded, unused = rows_send.shape
    tokens = normed_moe.shape[0]
    me = lax.axis_index("wide")
    line = lax.axis_index("narrow")
    barrier = pltpu.get_barrier_semaphore()
    greet(barrier, experts)
    right = (me, shifted(line, 1, shards))
    left = (me, shifted(line, shards - 1, shards))
    for near in (left, right):
        pl.semaphore_signal(barrier, inc=1, device_id=near, device_id_type=MESH)
    gate_slot[...] = jnp.zeros_like(gate_slot)

    def ring(k):
        source = first if k == 0 else weights.at[k - 1]
        return exchange(source, weights.at[k], ring_sem.at[0, k], ring_sem.at[1, k], right)

    keep = pltpu.make_async_copy(rows_send.at[me], received.at[me], own_sem)

    def move(j):
        to = paired(me, j, experts)
        return exchange(rows_send.at[to], received.at[me], send.at[j], recv.at[j], (to, line))

    @pl.loop(0, experts)
    def _(i):
        j = paired(i, experts - 2, experts)
        e = paired(me, j, experts)
        chosen = iota((padded, tokens), 0).astype(f32) == slot_row[pl.ds(e, 1), :]
        chosen = chosen.astype(f32).astype(bf16)
        rows_send[e] = dot(chosen, normed_moe[...]).astype(bf16)
        gate = gate_row[pl.ds(e, 1), :]
        high, middle = split2(gate)
        low = (gate - high.astype(f32) - middle.astype(f32)).astype(bf16)
        three = jnp.concatenate(
            [high.astype(f32), middle.astype(f32), low.astype(f32), jnp.zeros((5, tokens), f32)], axis=0
        )
        gate_slot[:, :padded] = dot_nt(three.astype(bf16), chosen)
        tail = rows_send[e, padded - 16 :, :].astype(f32)
        sub = iota(tail.shape, 0)
        for part in range(3):
            tail = jnp.where(sub == 13 + part, gate_slot[part : part + 1, :], tail)
        rows_send[e, padded - 16 :, :] = tail.astype(bf16)

        @pl.when(i == 0)
        def _():
            pl.semaphore_wait(barrier, experts + 1)
            ring(0).start()

        @pl.when(j != 0)
        def _():
            move(j).start()

        @pl.when(j == 0)
        def _():
            keep.start()

    keep.wait()
    for k in range(shards - 2):
        ring(k).wait()
        if k + 1 < shards - 2:
            ring(k + 1).start()

    @pl.loop(1, experts)
    def _(j):
        move(j).wait()


def dispatch(slot_row, gate_row, normed_moe, first, shards, padded):
    experts, tokens = slot_row.shape
    vmem = pl.BlockSpec(memory_space=pltpu.VMEM)
    anywhere = pl.BlockSpec(memory_space=pl.ANY)
    dma = pltpu.SemaphoreType.DMA
    return pl.pallas_call(
        functools.partial(dispatch_kernel, shards),
        in_specs=[vmem, vmem, vmem, anywhere],
        out_specs=(anywhere, anywhere),
        out_shape=(
            jax.ShapeDtypeStruct((experts, padded, D), bf16),
            jax.ShapeDtypeStruct((shards - 2,) + first.shape, bf16),
        ),
        scratch_shapes=[
            pltpu.VMEM((experts, padded, D), bf16),
            pltpu.VMEM((8, D), f32),
            dma((experts,)),
            dma((experts,)),
            dma,
            dma((2, shards - 2)),
        ],
        compiler_params=pltpu.CompilerParams(
            vmem_limit_bytes=40 * MIB, collective_id=3, has_side_effects=True
        ),
        cost_estimate=pl.CostEstimate(
            flops=20 * experts * padded * tokens * D, bytes_accessed=6 * MIB, transcendentals=0
        ),
        name="dispatch",
    )(slot_row, gate_row, normed_moe, first)


def expert_kernel(capacity, sources, shards, received, gz, gathered_in, out_own, out_first, out_rest, *refs):
    returned, back, ring, grads = refs[:4]
    rows, scaled, rows_t, gz_t, act, gpre, out_sum, back_sum, out_low, back_low, ring_out, ring_in = refs[4:16]
    out_send, out_recv, back_send, back_recv, own_sem, ring_sem = refs[16:]
    padded = rows.shape[1]
    hidden = act.shape[2]
    me = lax.axis_index("wide")
    line = lax.axis_index("narrow")
    right = (me, shifted(line, 1, shards))
    left = (me, shifted(line, shards - 1, shards))
    barrier = pltpu.get_barrier_semaphore()
    greet(barrier, sources)
    for near in (left, right):
        pl.semaphore_signal(barrier, inc=1, device_id=near, device_id_type=MESH)

    def sends(j):
        to = (paired(me, j, sources), line)
        return (
            exchange(out_low.at[to[0]], returned.at[me], out_send.at[j], out_recv.at[j], to),
            exchange(back_low.at[to[0]], back.at[me], back_send.at[j], back_recv.at[j], to),
        )

    def block(j):
        s = paired(me, j, sources)
        rows[s] = received[s]
        tail = received[s, padded - 16 :, :].astype(f32)
        gate = tail[13:14] + tail[14:15] + tail[15:16]
        gate = jnp.transpose(jnp.broadcast_to(gate, (LANES, D)))[:padded, :1]
        live = iota((padded, 1), 0) < capacity
        scaled[s] = (jnp.where(live, gate, 0.0) * gz[s].astype(f32)).astype(bf16)
        live16 = iota((16, 1), 0) < 16 - (padded - capacity)
        rows[s, padded - 16 :, :] = jnp.where(live16, tail, 0.0).astype(bf16)
        for c in range(shards):
            w_in = gathered_in[shifted(line, shards - c, shards)]
            w_out = out_rest[c - 2] if c > 1 else (out_first[...] if c else out_own[...])
            pre = dot(rows[s], w_in)
            phi, slope = gelu_parts(pre)
            act_low = (pre * phi).astype(bf16)
            act[c, pl.ds(pl.multiple_of(s * padded, 16), padded), :] = act_low
            grad_pre = (dot_nt(scaled[s], w_out) * (phi + slope)).astype(bf16)
            gpre[c, pl.ds(pl.multiple_of(s * padded, 16), padded), :] = grad_pre
            result = dot(act_low, w_out)
            grad_rows = dot_nt(grad_pre, w_in)
            if c > 0:
                result = result + out_sum[...]
                grad_rows = grad_rows + back_sum[...]
            if c < shards - 1:
                out_sum[...] = result
                back_sum[...] = grad_rows
            else:
                out_low[s] = result.astype(bf16)
                back_low[s] = grad_rows.astype(bf16)

    keep = (
        pltpu.make_async_copy(out_low.at[me], returned.at[me], own_sem.at[0]),
        pltpu.make_async_copy(back_low.at[me], back.at[me], own_sem.at[1]),
    )

    @pl.loop(0, sources)
    def _(i):
        j = paired(i, sources - 2, sources)
        block(j)

        @pl.when(i == 0)
        def _():
            pl.semaphore_wait(barrier, sources + 1)

        @pl.when(j != 0)
        def _():
            for copy in sends(j):
                copy.start()

        @pl.when(j == 0)
        def _():
            for copy in keep:
                copy.start()

    for s in range(sources):
        rows_t[:, s * padded : (s + 1) * padded] = jnp.transpose(rows[s])
        gz_t[:, s * padded : (s + 1) * padded] = jnp.transpose(scaled[s])
    def weight_grads(c):
        return dot(rows_t[...], gpre[c]).astype(bf16), dot(gz_t[...], act[c]).astype(bf16)

    ring_out[:D, :], ring_out[D:, :] = weight_grads(1)
    step = exchange(ring_out, ring_in, ring_sem.at[0], ring_sem.at[1], right)
    step.start()
    for c in range(3, shards):
        grads[c - 2, :D, :], grads[c - 2, D:, :] = weight_grads(c)
    grads[0, :D, :], grads[0, D:, :] = weight_grads(0)
    second = weight_grads(2)
    for copy in keep:
        copy.wait()
    step.wait()
    for half in range(2):
        span = slice(half * D, half * D + D)
        ring[span, :] = (ring_in[span, :].astype(f32) + second[half].astype(f32)).astype(bf16)

    @pl.loop(1, sources)
    def _(j):
        for copy in sends(j):
            copy.wait()


def experts_apply(rows, gz, gathered_in, out_own, out_first, out_rest, capacity):
    sources, padded, unused = rows.shape
    shards, unused, hidden = gathered_in.shape
    total = sources * padded
    vmem = pl.BlockSpec(memory_space=pltpu.VMEM)
    anywhere = pl.BlockSpec(memory_space=pl.ANY)
    dma = pltpu.SemaphoreType.DMA
    return pl.pallas_call(
        functools.partial(expert_kernel, capacity, sources, shards),
        in_specs=[vmem] * 6,
        out_specs=(anywhere, anywhere, vmem, vmem),
        out_shape=(
            jax.ShapeDtypeStruct(rows.shape, bf16),
            jax.ShapeDtypeStruct(rows.shape, bf16),
            jax.ShapeDtypeStruct((2 * D, hidden), bf16),
            jax.ShapeDtypeStruct((shards - 2, 2 * D, hidden), bf16),
        ),
        scratch_shapes=[
            pltpu.VMEM(rows.shape, bf16),
            pltpu.VMEM(rows.shape, bf16),
            pltpu.VMEM((D, total), bf16),
            pltpu.VMEM((D, total), bf16),
            pltpu.VMEM((shards, total, hidden), bf16),
            pltpu.VMEM((shards, total, hidden), bf16),
            pltpu.VMEM((padded, D), f32),
            pltpu.VMEM((padded, D), f32),
            pltpu.VMEM(rows.shape, bf16),
            pltpu.VMEM(rows.shape, bf16),
            pltpu.VMEM((2 * D, hidden), bf16),
            pltpu.VMEM((2 * D, hidden), bf16),
            dma((sources,)),
            dma((sources,)),
            dma((sources,)),
            dma((sources,)),
            dma((2,)),
            dma((2,)),
        ],
        compiler_params=pltpu.CompilerParams(
            vmem_limit_bytes=60 * MIB, collective_id=1, has_side_effects=True
        ),
        cost_estimate=pl.CostEstimate(
            flops=12 * total * D * hidden * shards, bytes_accessed=20 * MIB, transcendentals=0
        ),
        name="experts",
    )(rows, gz, gathered_in, out_own, out_first, out_rest)


def backward_kernel(
    experts,
    windows,
    seg,
    w_proj,
    gain_moe,
    w_router,
    slot_col,
    cot,
    packed_in,
    context_in,
    lse,
    residual,
    normed_moe,
    gates,
    returned,
    back,
    counts,
    mixed_out,
    grad_residual_out,
    grad_packed,
    grad_proj,
    small,
    packed,
    context,
    mixed,
    grad_residual,
    hot,
    seg_col,
    seg_row,
    router,
    grad_attn,
    grad_context,
    grad_logits,
    grad_k,
    grad_v,
    sems,
):
    tokens = cot.shape[0]
    slots_all, padded = returned.shape[0] * returned.shape[1], returned.shape[1]
    reads = (
        pltpu.make_async_copy(packed_in, packed, sems.at[0]),
        pltpu.make_async_copy(context_in, context, sems.at[1]),
    )
    writes = (
        pltpu.make_async_copy(mixed, mixed_out, sems.at[2]),
        pltpu.make_async_copy(grad_residual, grad_residual_out, sems.at[3]),
    )
    for read in reads:
        read.start()
    seg_row[...] = seg[...].astype(f32)
    seg_col[...] = jnp.transpose(jnp.broadcast_to(seg_row[...], (LANES, tokens)))
    router[...] = jnp.zeros_like(router)
    router[:, :experts] = w_router[...]
    small[...] = jnp.zeros_like(small)
    small[2:4, :LANES] = counts[:2, :]

    @pl.loop(0, tokens // TILE)
    def _(i):
        rows = pl.ds(pl.multiple_of(i * TILE, TILE), TILE)
        grad_z = cot[rows, :].astype(f32)
        probs = gates[rows, :]
        slots = slot_col[rows, :]
        lane = iota((TILE, LANES), 1)
        rest = residual[rows, :]
        twice = probs + pltpu.roll(probs, experts, axis=1)
        place = jnp.where(lane < experts, lane, lane - experts).astype(f32) * float(padded)
        total = rest
        grad_gates = jnp.zeros((TILE, LANES), f32)
        spots = iota((TILE, slots_all), 1).astype(f32)
        picks = []
        for k in range(TOP):
            mine = (slots >= 0.0) & (lane >= k * experts) & (lane < (k + 1) * experts)
            spot = jnp.sum(jnp.where(mine, place + slots + 1.0, 0.0), axis=1, keepdims=True) - 1.0
            hot[k * TILE : (k + 1) * TILE, :] = (spots == spot).astype(f32).astype(bf16)
            picks.append(mine)
        back_total = dot(hot[:TILE, :] + hot[TILE:, :], back[...].reshape(slots_all, D))
        results = dot(hot[...], returned[...].reshape(slots_all, D))
        for k in range(TOP):
            result = results[k * TILE : (k + 1) * TILE]
            total = total + jnp.sum(jnp.where(picks[k], twice, 0.0), axis=1, keepdims=True) * result
            inner = jnp.sum(result * grad_z, axis=1, keepdims=True)
            grad_gates = grad_gates + jnp.where(picks[k], inner, 0.0)
        grad_gates = grad_gates + pltpu.roll(grad_gates, LANES - experts, axis=1)
        grad_gates = jnp.where(lane < experts, grad_gates, 0.0)
        mixed[rows, :] = total.astype(bf16)
        gate_inner = jnp.sum(probs * grad_gates, axis=1, keepdims=True)
        high, low = split2(probs * (grad_gates - gate_inner))
        grad_logits[rows, :LANES] = high
        grad_logits[rows, LANES:] = low
        grad_normed = back_total + dot_nt(high, router[...]) + dot_nt(low, router[...])
        normal, inverse = norm_parts(rest)
        grad_norm, grad_gain = norm_back(grad_normed, gain_moe[...], normal, inverse)
        small[1:2, :] += grad_gain
        grad_rest = grad_z + grad_norm
        grad_residual[rows, :] = grad_rest
        attn = grad_rest.astype(bf16)
        grad_attn[rows, :] = attn
        grad_context[rows, :] = dot_nt(attn, w_proj[...]).astype(bf16)

    for write in writes:
        write.start()
    for read in reads:
        read.wait()
    both = dot_tn(normed_moe[...], grad_logits[...])
    both = jnp.transpose(both[:, :LANES] + both[:, LANES:])
    small[8:, :] = both[:experts]
    grad_proj[...] = dot_tn(context[...], grad_attn[...])
    grad_k[...] = jnp.zeros_like(grad_k)
    grad_v[...] = jnp.zeros_like(grad_v)

    @pl.loop(0, tokens // QB)
    def _(block):
        query = pl.multiple_of(block * QB, QB)

        def body(low, width):
            bias = window_bias(seg_col, seg_row, low, width, query)
            spans = [slice(pair * PAIR, (pair + 1) * PAIR) for pair in range(PAIRS)]
            keys = pl.ds(low, width)
            queries = [
                (stack_heads(packed[pl.ds(query, QB), span]) * HEAD ** (-0.5)).astype(bf16) for span in spans
            ]
            grads = [stack_heads(grad_context[pl.ds(query, QB), span]) for span in spans]
            probs = []
            grad_probs = []
            for pair, span in enumerate(spans):
                k = packed[keys, D + span.start : D + span.stop]
                v = packed[keys, 2 * D + span.start : 2 * D + span.stop]
                probs.append(jnp.exp(dot_nt(k, queries[pair]) + bias - lse[pl.ds(block, 1), pair, :]))
                grad_probs.append(dot_nt(v, grads[pair]))
            grad_scores = []
            for pair, span in enumerate(spans):
                grad_v[keys, span] += dot(probs[pair].astype(bf16), grads[pair])
                weighted = probs[pair] * grad_probs[pair]
                inner = jnp.sum(weighted, axis=0, keepdims=True)
                grad_scores.append((weighted - probs[pair] * inner).astype(bf16))
            for pair, span in enumerate(spans):
                k = packed[keys, D + span.start : D + span.stop]
                grad_k[keys, span] += dot(grad_scores[pair], queries[pair])
                grad_q = unstack_cols(dot_tn(k, grad_scores[pair])) * HEAD ** (-0.5)
                grad_packed[pl.ds(query, QB), span] = grad_q.astype(bf16)

        by_window(windows, block, body)

    @pl.loop(0, tokens // TILE)
    def _(i):
        rows = pl.ds(pl.multiple_of(i * TILE, TILE), TILE)
        grad_packed[rows, D : 2 * D] = grad_k[rows, :].astype(bf16)
        grad_packed[rows, 2 * D :] = grad_v[rows, :].astype(bf16)

    for write in writes:
        write.wait()


def backward(experts, windows, *operands):
    cot = operands[5]
    returned = operands[-3]
    tokens = cot.shape[0]
    vmem = pl.BlockSpec(memory_space=pltpu.VMEM)
    anywhere = pl.BlockSpec(memory_space=pl.ANY)
    return pl.pallas_call(
        functools.partial(backward_kernel, experts),
        in_specs=[pl.BlockSpec(memory_space=pltpu.SMEM)] + [vmem] * 6 + [anywhere] * 2 + [vmem] * (len(operands) - 8),
        out_specs=[anywhere, anywhere, vmem, vmem, vmem],
        out_shape=(
            jax.ShapeDtypeStruct((tokens, D), bf16),
            jax.ShapeDtypeStruct((tokens, D), f32),
            jax.ShapeDtypeStruct((tokens, 3 * D), bf16),
            jax.ShapeDtypeStruct((D, D), f32),
            jax.ShapeDtypeStruct((8 + experts, D), f32),
        ),
        scratch_shapes=[
            pltpu.VMEM((tokens, 3 * D), bf16),
            pltpu.VMEM((tokens, D), bf16),
            pltpu.VMEM((tokens, D), bf16),
            pltpu.VMEM((tokens, D), f32),
            pltpu.VMEM((TOP * TILE, returned.shape[0] * returned.shape[1]), bf16),
            pltpu.VMEM((tokens, LANES), f32),
            pltpu.VMEM((1, tokens), f32),
            pltpu.VMEM((D, LANES), bf16),
            pltpu.VMEM((tokens, D), bf16),
            pltpu.VMEM((tokens, D), bf16),
            pltpu.VMEM((tokens, 2 * LANES), bf16),
            pltpu.VMEM((tokens, D), f32),
            pltpu.VMEM((tokens, D), f32),
            pltpu.SemaphoreType.DMA((4,)),
        ],
        compiler_params=pltpu.CompilerParams(vmem_limit_bytes=60 * MIB),
        cost_estimate=pl.CostEstimate(
            flops=30 * 1024 * MIB, bytes_accessed=30 * MIB, transcendentals=4 * MIB
        ),
        name="attention_backward",
    )(windows, *operands)


def shared_kernel(
    chips,
    planes,
    normed_attn,
    grad_packed,
    grad_proj,
    partial,
    tok,
    grad_residual,
    gain_attn,
    w_qkv,
    summed,
    small,
    grad_tokens,
    normed_t,
    half,
    core_out,
    core_in,
    chip_out,
    chip_in,
    plane_own,
    plane_out,
    plane_in,
    small_own,
    small_core,
    small_chip,
    small_plane,
    core_sem,
    chip_sem,
    plane_sem,
    plane_sem2,
    chip_sem2,
    core_sem2,
    small_sem,
    small_chip_sem,
    small_plane_sem,
):
    tokens = tok.shape[0]
    columns = summed.shape[2]
    part = D // columns if columns < D else 1
    wide = lax.axis_index("wide")
    plane = lax.axis_index("narrow")
    core = lax.rem(wide, 2)
    chip = wide // 2
    share = D // (2 * chips)
    partner = (chip * 2 + 1 - core, plane)
    mine = pl.ds(pl.multiple_of(core * (D // 2), D // 2), D // 2)
    other = pl.ds(pl.multiple_of((1 - core) * (D // 2), D // 2), D // 2)
    chunk = pl.ds(pl.multiple_of(core * (D // 2) + chip * share, share), share)
    own_chunk = pl.ds(pl.multiple_of(chip * share, share), share)

    def chip_at(j):
        to = shifted(chip, j, chips)
        return to, (to * 2 + core, plane)

    def plane_at(j):
        to = shifted(plane, j, planes)
        return to, (wide, to)

    barrier = pltpu.get_barrier_semaphore()
    pl.semaphore_signal(barrier, inc=1, device_id=partner, device_id_type=MESH)

    @pl.loop(1, chips)
    def _(j):
        pl.semaphore_signal(barrier, inc=1, device_id=chip_at(j)[1], device_id_type=MESH)

    @pl.loop(1, planes)
    def _(j):
        pl.semaphore_signal(barrier, inc=1, device_id=plane_at(j)[1], device_id_type=MESH)

    def core_copy(n):
        return exchange(core_out.at[n], core_in.at[n], core_sem.at[0, n], core_sem.at[1, n], partner)

    def chip_copy(n, j):
        to, device = chip_at(j)
        rows = pl.ds(pl.multiple_of(to * share, share), share)
        return exchange(
            chip_out.at[n, rows], chip_in.at[j, n], chip_sem.at[0, j, n], chip_sem.at[1, j, n], device
        )

    def plane_copy(j):
        to, device = plane_at(j)
        return exchange(plane_out.at[to], plane_in.at[j], plane_sem.at[0, j], plane_sem.at[1, j], device)

    def plane_back(j):
        spot = summed.at[plane, chunk]
        return exchange(spot, spot, plane_sem2.at[0, j], plane_sem2.at[1, j], plane_at(j)[1])

    def column_of(i):
        return shifted(plane, planes - i, planes)

    def chip_back(i, j):
        spot = summed.at[column_of(i), chunk]
        return exchange(spot, spot, chip_sem2.at[0, j, i], chip_sem2.at[1, j, i], chip_at(j)[1])

    def core_back(i):
        spot = summed.at[column_of(i), mine]
        return exchange(spot, spot, core_sem2.at[0, i], core_sem2.at[1, i], partner)

    def small_core_copy():
        return exchange(small_own, small_core, small_sem.at[0], small_sem.at[1], partner)

    def small_chip_copy(j):
        return exchange(
            small_chip.at[chip],
            small_chip.at[chip],
            small_chip_sem.at[0, j],
            small_chip_sem.at[1, j],
            chip_at(j)[1],
        )

    def small_plane_copy(j):
        return exchange(
            small_plane.at[plane],
            small_plane.at[plane],
            small_plane_sem.at[0, j],
            small_plane_sem.at[1, j],
            plane_at(j)[1],
        )

    order = [(3, p) for p in range(part)] + [(t, p) for t in range(3) for p in range(part)]
    normed_t[...] = jnp.transpose(normed_attn[...])
    for t, p in order:
        n = t * part + p
        if t == 3:
            half[n] = grad_proj[mine, p * columns : (p + 1) * columns]
            core_out[n] = grad_proj[other, p * columns : (p + 1) * columns].astype(bf16)
        else:
            right = grad_packed[:, n * columns : (n + 1) * columns]
            core_out[n] = dot(normed_t[other, :], right).astype(bf16)
        if (t, p) == order[0]:
            pl.semaphore_wait(barrier, chips + planes - 1)
        core_copy(n).start()
        if t < 3:
            half[n] = dot(normed_t[mine, :], right)
    for t, p in order:
        n = t * part + p
        core_copy(n).wait_recv()
        half[n] = half[n] + core_in[n].astype(f32)
        chip_out[n] = half[n].astype(bf16)

        @pl.loop(1, chips)
        def _(j):
            chip_copy(n, j).start()

    small_own[...] = partial[...]

    @pl.loop(0, tokens // TILE)
    def _(i):
        rows = pl.ds(pl.multiple_of(i * TILE, TILE), TILE)
        grad_normed = dot_nt(grad_packed[rows, :], w_qkv[...])
        normal, inverse = norm_parts(tok[rows, :].astype(f32))
        grad_norm, grad_gain = norm_back(grad_normed, gain_attn[...], normal, inverse)
        small_own[0:1, :] += grad_gain
        grad_tokens[rows, :] = grad_residual[rows, :] + grad_norm

    small_core_copy().start()
    for t, p in order:
        n = t * part + p
        total = half[n, own_chunk, :]
        for j in range(1, chips):
            chip_copy(n, j).wait_recv()
            total = total + chip_in[j, n].astype(f32)
        plane_out[n] = total.astype(bf16)

        @pl.when(n == plane)
        def _():
            plane_own[...] = total

        @pl.when(n != plane)
        def _():
            plane_copy(lax.rem(n + planes - plane, planes)).start()

    small_core_copy().wait_recv()
    small_chip[chip] = small_own[...] + small_core[...]

    @pl.loop(1, chips)
    def _(j):
        small_chip_copy(j).start()

    total = plane_own[...]
    for j in range(1, planes):
        plane_copy(j).wait_recv()
        total = total + plane_in[j].astype(f32)
    summed[plane, chunk, :] = total.astype(bf16)

    @pl.loop(1, planes)
    def _(j):
        plane_back(j).start()

    @pl.loop(1, chips)
    def _(j):
        small_chip_copy(j).wait_recv()

    total = small_chip[0]
    for c in range(1, chips):
        total = total + small_chip[c]
    small_plane[plane] = total

    @pl.loop(1, planes)
    def _(j):
        small_plane_copy(j).start()

    for i in range(planes):
        if i > 0:
            plane_back(i).wait_recv()

        @pl.loop(1, chips)
        def _(j):
            chip_back(i, j).start()

    for i in range(planes):

        @pl.loop(1, chips)
        def _(j):
            chip_back(i, j).wait_recv()

        core_back(i).start()

    @pl.loop(1, planes)
    def _(j):
        small_plane_copy(j).wait_recv()

    total = small_plane[0]
    for c in range(1, planes):
        total = total + small_plane[c]
    small[...] = total
    for i in range(planes):
        core_back(i).wait()
        core_copy(i).wait_send()

        @pl.loop(1, chips)
        def _(j):
            chip_back(i, j).wait_send()
            chip_copy(i, j).wait_send()

    @pl.loop(1, planes)
    def _(j):
        plane_back(j).wait_send()
        plane_copy(j).wait_send()
        small_plane_copy(j).wait_send()

    @pl.loop(1, chips)
    def _(j):
        small_chip_copy(j).wait_send()

    small_core_copy().wait_send()


def shared_gradients(*operands):
    normed_attn, unused, unused, partial = operands[:4]
    tokens = normed_attn.shape[0]
    chips = lax.axis_size("wide") // 2
    planes = lax.axis_size("narrow")
    columns = 4 * D // planes
    share = D // (2 * chips)
    rows = partial.shape[0]
    dma = pltpu.SemaphoreType.DMA
    return pl.pallas_call(
        functools.partial(shared_kernel, chips, planes),
        out_shape=(
            jax.ShapeDtypeStruct((planes, D, columns), bf16),
            jax.ShapeDtypeStruct((rows, D), f32),
            jax.ShapeDtypeStruct((tokens, D), f32),
        ),
        scratch_shapes=[
            pltpu.VMEM((D, tokens), bf16),
            pltpu.VMEM((planes, D // 2, columns), f32),
            pltpu.VMEM((planes, D // 2, columns), bf16),
            pltpu.VMEM((planes, D // 2, columns), bf16),
            pltpu.VMEM((planes, D // 2, columns), bf16),
            pltpu.VMEM((chips, planes, share, columns), bf16),
            pltpu.VMEM((share, columns), f32),
            pltpu.VMEM((planes, share, columns), bf16),
            pltpu.VMEM((planes, share, columns), bf16),
            pltpu.VMEM((rows, D), f32),
            pltpu.VMEM((rows, D), f32),
            pltpu.VMEM((chips, rows, D), f32),
            pltpu.VMEM((planes, rows, D), f32),
            dma((2, planes)),
            dma((2, chips, planes)),
            dma((2, planes)),
            dma((2, planes)),
            dma((2, chips, planes)),
            dma((2, planes)),
            dma((2,)),
            dma((2, chips)),
            dma((2, planes)),
        ],
        compiler_params=pltpu.CompilerParams(
            vmem_limit_bytes=50 * MIB, collective_id=2, has_side_effects=True
        ),
        cost_estimate=pl.CostEstimate(
            flops=12 * tokens * D * D, bytes_accessed=16 * MIB, transcendentals=0
        ),
        name="shared_gradients",
    )(*operands)


def finish_kernel(experts, summed, ring, own, small, tokens_in, qkv, proj, grad_in, grad_out, rest, router, tokens_out, sem):
    copy = pltpu.make_async_copy(tokens_in, tokens_out, sem)
    copy.start()
    planes, unused, columns = summed.shape
    for n in range(planes):
        start = n * columns
        if start < 3 * D:
            qkv[:, start : start + columns] = summed[n].astype(f32)
        else:
            proj[:, start - 3 * D : start - 3 * D + columns] = summed[n].astype(f32)
    total = ring[...].astype(f32) + own[...].astype(f32)
    grad_in[0] = total[:D, :]
    grad_out[0] = jnp.transpose(total[D:, :])
    rest[...] = small[:8, :]
    router[...] = jnp.transpose(jnp.concatenate([small[8:, :], jnp.zeros((LANES - experts, D), f32)], axis=0))[
        :, :experts
    ]
    copy.wait()


def finish(experts, summed, ring, own, small, tokens_in):
    hidden = own.shape[1]
    vmem = pl.BlockSpec(memory_space=pltpu.VMEM)
    anywhere = pl.BlockSpec(memory_space=pl.ANY)
    return pl.pallas_call(
        functools.partial(finish_kernel, experts),
        in_specs=[vmem, vmem, vmem, vmem, anywhere],
        out_specs=[vmem] * 6 + [anywhere],
        out_shape=(
            jax.ShapeDtypeStruct((D, 3 * D), f32),
            jax.ShapeDtypeStruct((D, D), f32),
            jax.ShapeDtypeStruct((1, D, hidden), f32),
            jax.ShapeDtypeStruct((1, hidden, D), f32),
            jax.ShapeDtypeStruct((8, D), f32),
            jax.ShapeDtypeStruct((D, experts), f32),
            jax.ShapeDtypeStruct(tokens_in.shape, f32),
        ),
        scratch_shapes=[pltpu.SemaphoreType.DMA],
        compiler_params=pltpu.CompilerParams(vmem_limit_bytes=40 * MIB),
        cost_estimate=pl.CostEstimate(flops=0, bytes_accessed=14 * MIB, transcendentals=0),
        name="finish",
    )(summed, ring, own, small, tokens_in)


def per_device(
    tokens,
    segment_ids,
    expert_picks,
    priority_ranks,
    gain_attn,
    w_qkv,
    w_proj,
    gain_moe,
    w_router,
    w_in,
    w_out,
    cotangent,
):
    experts = w_router.shape[1]
    capacity = (21 * TOP * TOK_DEV + 20 * experts - 1) // (20 * experts)
    padded = (capacity + 3 + 15) // 16 * 16
    gain_attn = gain_attn.reshape(1, D)
    gain_moe = gain_moe.reshape(1, D)
    seg = segment_ids.reshape(1, SEQ)
    first = jnp.sum((segment_ids[None, :] < segment_ids[0::QB, None]).astype(jnp.int32), axis=1)
    after = jnp.sum((segment_ids[None, :] <= segment_ids[QB - 1 :: QB, None]).astype(jnp.int32), axis=1)
    low = jnp.minimum(first // 16 * 16, SEQ - WINDOW)
    fits = (after - low <= WINDOW).astype(jnp.int32)
    windows = jnp.concatenate([low, fits])

    line = lax.axis_size("narrow")
    ring_steps = [(i, (i + 1) % line) for i in range(line)]
    together = lax.optimization_barrier

    def pass_on(values):
        return lax.ppermute(values, "narrow", ring_steps)

    out_own = w_out[0]
    out_first = pass_on(out_own)
    gathered_in = lax.all_gather(w_in[0], "narrow", axis=0)
    slot_col, slot_row, counts, gz_send = route(
        expert_picks, priority_ranks, cotangent, experts, capacity, padded
    )
    gz = lax.all_to_all(gz_send, "wide", split_axis=0, concat_axis=0, tiled=True)
    normed_attn, packed, context, lse, residual, normed_moe, gates, gate_row = forward(
        windows, tokens, seg, gain_attn, w_qkv, w_proj, gain_moe, w_router
    )
    rows, out_rest = dispatch(slot_row, gate_row, normed_moe, out_first, line, padded)
    returned, back, ring, grads = experts_apply(rows, gz, gathered_in, out_own, out_first, out_rest, capacity)
    ring = pass_on(ring)
    mixed, grad_residual, grad_packed, grad_proj, partial = backward(
        experts,
        windows,
        seg,
        w_proj,
        gain_moe,
        w_router,
        slot_col,
        cotangent,
        packed,
        context,
        lse,
        residual,
        normed_moe,
        gates,
        returned,
        back,
        counts,
    )
    ring, grad_packed = together((ring, grad_packed))
    for k in range(1, line - 2):
        ring = pass_on((ring.astype(f32) + grads[k].astype(f32)).astype(bf16))
    summed, small, grad_tokens = shared_gradients(
        normed_attn, grad_packed, grad_proj, partial, tokens, grad_residual, gain_attn, w_qkv
    )
    grad_qkv, grad_proj, grad_in, grad_out, rest, grad_router, grad_tokens = finish(
        experts, summed, ring, grads[0], small, grad_tokens
    )
    counted = rest[2:4, :experts].astype(jnp.int32)
    return (
        mixed,
        grad_tokens,
        rest[0],
        grad_qkv,
        grad_proj,
        rest[1],
        grad_router,
        grad_in,
        grad_out,
        counted[0],
        counted[1] - counted[0],
    )


def solution(mesh):
    both = ("wide", "narrow")
    placed = (
        P(both, None),
        P(both),
        P(both, None),
        P(both, None),
        P(),
        P(),
        P(),
        P(),
        P(),
        P("wide", None, "narrow"),
        P("wide", "narrow", None),
        P(both, None),
    )
    return jax.shard_map(
        per_device,
        mesh=mesh,
        in_specs=placed,
        out_specs=(
            P(both, None),
            P(both, None),
            P(),
            P(),
            P(),
            P(),
            P(),
            P("wide", None, "narrow"),
            P("wide", "narrow", None),
            P(),
            P(),
        ),
        check_vma=False,
    )
```

profile of v0, /device:TPU:0, one launch (start us, length us, event | category | flops | bytes accessed | tf_op | source)
XLA Modules:
  0.0 246.7 jit_solution(15496130042534252413)
XLA Ops:
  7.2 0.7 all-gather.2.cloned.1.call-update
  7.9 3.1 %collective-permute-start = (bf16[512,512]{1,0:T(8,128)(2,1)}, bf16[512,512]{1,0:T(8,128)(2,1)S(1)}, u32[]{:S(2)}, u32[]{:S(2)}) collective-permute-start(bf16[512,512]{1,0:T(8,128)(2,1)} %bitcast.22), channel_id=1, source_target_pairs={{0,1},{1,2},{2,3},{3,0},{4,5},{5,6},{6,7},{7,4},{8,9},{9,10},{10,1... | collective-permute-start | bytes 1572872 | tf_op jit(solution)/shard_map/ppermute | solution.py:1154
  11.0 0.9 copy.31.picks
  11.9 1.2 copy-done.2
  13.1 0.7 copy-done.5
  13.8 6.3 %route.1 = (f32[1024,128]{1,0:T(8,128)S(1)}, f32[8,1024]{1,0:T(8,128)S(1)}, f32[8,128]{1,0:T(8,128)S(1)}, bf16[8,272,512]{2,1,0:T(8,128)(2,1)}) custom-call(s32[1024,2]{1,0:T(8,128)S(1)} %copy.31.picks, s32[1,1024]{1,0:T(1,128)S(1)} %copy-done.5, bf16[1024,512]{1,0:T(8,128)(2,1)S(1)} %copy-done.2), custom_call_target="tpu_custom_call" | custom-call | flops 2281701376 | bytes 6291456 | tf_op jit(solution)/shard_map/route/pallas_call | solution.py:109
  20.1 0.8 copy-done.9
  20.9 0.6 copy-done.14
  21.5 3.9 %all-to-all-start = ((bf16[8,272,512]{2,1,0:T(8,128)(2,1)}), bf16[8,272,512]{2,1,0:T(8,128)(2,1)S(1)}, u32[]{:S(2)}, u32[]{:S(2)}) async-start(bf16[8,272,512]{2,1,0:T(8,128)(2,1)} %get-tuple-element.56), calls=%async_computation | async-start | bytes 4456448 | tf_op jit(solution)/shard_map/all_to_all | solution.py:1162
  25.8 0.8 copy.33.w_router
  26.6 0.6 pad_add_fusion.windows
  27.2 19.1 %attention_forward.1 = (bf16[1024,512]{1,0:T(8,128)(2,1)}, bf16[1024,1536]{1,0:T(8,128)(2,1)}, bf16[1024,512]{1,0:T(8,128)(2,1)}, f32[8,4,256]{2,1,0:T(4,128)}, ...) custom-call(s32[16]{0:T(128)} %pad_add_fusion.windows, ...), custom_call_target="tpu_custom_call" | custom-call | flops 8589934592 | bytes 16777216 | tf_op jit(solution)/shard_map/attention_forward/pallas_call | solution.py:268
  46.3 1.4 copy-done.11
  47.7 0.8 copy-done.15
  48.5 35.6 %dispatch.1 = (bf16[8,272,512]{2,1,0:T(8,128)(2,1)S(1)}, bf16[2,512,512]{2,1,0:T(8,128)(2,1)S(1)}) custom-call(f32[8,1024]{1,0:T(8,128)S(1)} %get-tuple-element.53.slot_row, f32[8,1024]{1,0:T(8,128)S(1)} %copy-done.15, bf16[1024,512]{1,0:T(8,128)(2,1)S(1)} %copy-done.11, bf16[512,512]{1,0:T(8,128)(2,1)S(1)} %collective-permute-done.first.out_first), custom_call_target="tpu_custom_call" | custom-call | flops 22817013760 | bytes 6291456 | tf_op jit(solution)/shard_map/dispatch/pallas_call | solution.py:409
  84.2 1.4 copy-done.12
  85.6 1.0 copy-done.13
  86.6 1.4 copy-done.16
  87.9 59.3 %experts.1 = (bf16[8,272,512]{2,1,0:T(8,128)(2,1)}, bf16[8,272,512]{2,1,0:T(8,128)(2,1)}, bf16[1024,512]{1,0:T(8,128)(2,1)}, bf16[2,1024,512]{2,1,0:T(8,128)(2,1)}) custom-call(bf16[8,272,512]{2,1,0:T(8,128)(2,1)} %copy-done.12, bf16[8,272,512]{2,1,0:T(8,128)(2,1)} %copy-done.16, bf16[4,512,512]{2,1,0:T(8,128)(2,1)} %all-gather.2.cloned.1.call-done.gathered_in, ...), custom_call_target="tpu_custom_call" | custom-call | flops 27380416512 | bytes 20971520 | tf_op jit(solution)/shard_map/experts/pallas_call | solution.py:545
  147.2 0.6 collective-permute-start.1
  147.8 33.2 %attention_backward.1 = (bf16[1024,512]{1,0:T(8,128)(2,1)}, f32[1024,512]{1,0:T(8,128)}, bf16[1024,1536]{1,0:T(8,128)(2,1)}, f32[512,512]{1,0:T(8,128)}, f32[16,512]{1,0:T(8,128)}) custom-call(s32[16]{0:T(128)} %pad_add_fusion.windows, s32[1,1024]{1,0:T(1,128)} %bitcast.19, bf16[512,512]{1,0:T(8,128)(2,1)} %w_proj.3, f32[1,512]{1,0:T(1,128)} %bitcast.25, ...), custom_call_target="tpu_custom_call" | custom-call | flops 32212254720 | bytes 31457280 | tf_op jit(solution)/shard_map/attention_backward/pallas_call | solution.py:745
  181.1 0.3 fusion
  181.4 0.6 collective-permute-start.2
  182.3 0.3 copy-done.7
  182.6 0.3 copy-done.8
  182.9 47.9 %shared_gradients.1 = (bf16[4,512,512]{2,1,0:T(8,128)(2,1)}, f32[16,512]{1,0:T(8,128)S(1)}, f32[1024,512]{1,0:T(8,128)}) custom-call(bf16[1024,512]{1,0:T(8,128)(2,1)S(1)} %copy-done.7, bf16[1024,1536]{1,0:T(8,128)(2,1)} %get-tuple-element.65.grad_packed, f32[512,512]{1,0:T(8,128)S(1)} %copy-done.8, f32[16,512]{1,0:T(8,128)S(1)} %copy-done.10, ...), custom_call_target="tpu_custom_call" | custom-call | flops 3221225472 | bytes 16777216 | tf_op jit(solution)/shard_map/shared_gradients/pallas_call | solution.py:1038
  230.8 1.6 copy-done
  232.4 1.6 copy-done.1
  234.0 4.0 %finish.1 = (f32[512,1536]{1,0:T(8,128)}, f32[512,512]{1,0:T(8,128)}, f32[1,512,512]{2,1,0:T(8,128)}, f32[1,512,512]{2,1,0:T(8,128)}, f32[8,512]{1,0:T(8,128)S(1...) custom-call(bf16[4,512,512]{2,1,0:T(8,128)(2,1)S(1)} %copy-done, bf16[1024,512]{1,0:T(8,128)(2,1)S(1)} %collective-permute-done.2.ring, ...), custom_call_target="tpu_custom_call" | custom-call | bytes 14680064 | tf_op jit(solution)/shard_map/finish/pallas_call | solution.py:1103
  238.0 0.6 fusion.1
  238.6 0.5 bitcast_subtract_fusion
  239.1 0.7 copy.34
  (39 shorter events, 0.8 us)
Async XLA Ops:
  7.2 79.4 %all-gather.2.cloned.1.call-start = ((), (), s32[]{:S(2)}) async-start(), calls=%async_computation.1 | async-start | bytes 2621440 | tf_op jit(solution)/shard_map/all_gather | solution.py:1158
  7.9 38.4 %collective-permute-start = (bf16[512,512]{1,0:T(8,128)(2,1)}, bf16[512,512]{1,0:T(8,128)(2,1)S(1)}, u32[]{:S(2)}, u32[]{:S(2)}) collective-permute-start(bf16[512,512]{1,0:T(8,128)(2,1)} %bitcast.22), channel_id=1, source_target_pairs={{0,1},{1,2},{2,3},{3,0},{4,5},{5,6},{6,7},{7,4},{8,9},{9,10},{10,1... | collective-permute-start | bytes 1572872 | tf_op jit(solution)/shard_map/ppermute | solution.py:1154
  11.9 1.2 copy-start.2
  13.1 0.7 copy-start.5
  20.1 0.8 copy-start.9
  20.9 0.6 copy-start.14
  21.5 3.9 %copy-start.19 = (s32[1024]{0:T(1024)S(1)}, s32[1024]{0:T(1024)}, u32[]{:S(2)}) copy-start(s32[1024]{0:T(1024)} %param.13) | copy-start | bytes 12292
  21.5 4.3 %copy-start.18 = (bf16[512,8]{0,1:T(8,128)(2,1)S(1)}, bf16[512,8]{0,1:T(8,128)(2,1)}, u32[]{:S(2)}) copy-start(bf16[512,8]{0,1:T(8,128)(2,1)} %param.20) | copy-start | bytes 24580
  21.5 65.1 %all-to-all-start = ((bf16[8,272,512]{2,1,0:T(8,128)(2,1)}), bf16[8,272,512]{2,1,0:T(8,128)(2,1)S(1)}, u32[]{:S(2)}, u32[]{:S(2)}) async-start(bf16[8,272,512]{2,1,0:T(8,128)(2,1)} %get-tuple-element.56), calls=%async_computation | async-start | bytes 4456448 | tf_op jit(solution)/shard_map/all_to_all | solution.py:1162
  46.3 37.8 %copy-start.4 = (bf16[512,512]{1,0:T(8,128)(2,1)}, bf16[512,512]{1,0:T(8,128)(2,1)S(1)}, u32[]{:S(2)}) copy-start(bf16[512,512]{1,0:T(8,128)(2,1)S(1)} %collective-permute-done.first.out_first) | copy-start | bytes 1572868
  46.3 1.4 copy-start.11
  47.7 0.8 copy-start.15
  84.1 1.5 copy-start.12
  85.6 1.0 copy-start.13
  86.6 1.4 copy-start.16
  147.2 33.8 %collective-permute-start.1 = (bf16[1024,512]{1,0:T(8,128)(2,1)}, bf16[1024,512]{1,0:T(8,128)(2,1)S(1)}, u32[]{:S(2)}, u32[]{:S(2)}) collective-permute-start(bf16[1024,512]{1,0:T(8,128)(2,1)} %get-tuple-element.63), channel_id=1, source_target_pairs={{0,1},{1,2},{2,3},{3,0},{4,5},{5,6},{6,7},{7,4},{8,9},{9,10},{10,1... | collective-permute-start | bytes 3145736 | tf_op jit(solution)/shard_map/ppermute | solution.py:1154
  147.8 33.2 %copy-start.17 = (bf16[2,1024,512]{2,1,0:T(8,128)(2,1)S(1)}, bf16[2,1024,512]{2,1,0:T(8,128)(2,1)}, u32[]{:S(2)}) copy-start(bf16[2,1024,512]{2,1,0:T(8,128)(2,1)} %get-tuple-element.71) | copy-start | bytes 6291460
  181.0 1.2 copy-start.3
  181.0 1.2 copy-start.6
  181.0 1.5 copy-start.7
  181.1 1.8 copy-start.8
  181.1 1.8 copy-start.10
  181.4 49.4 %collective-permute-start.2 = (bf16[1024,512]{1,0:T(8,128)(2,1)S(1)}, bf16[1024,512]{1,0:T(8,128)(2,1)S(1)}, u32[]{:S(2)}, u32[]{:S(2)}) collective-permute-start(bf16[1024,512]{1,0:T(8,128)(2,1)S(1)} %fusion), channel_id=1, source_target_pairs={{0,1},{1,2},{2,3},{3,0},{4,5},{5,6},{6,7},{7,4},{8,9},{9,10},{10,1... | collective-permute-start | bytes 3145736 | tf_op jit(solution)/shard_map/ppermute | solution.py:1154
  230.8 1.6 copy-start
  232.4 1.6 copy-start.1
Sparse Core Ops, SparseCore 0:
  9.6 54.5 all-gather.1
where the time goes:
time: 252 us; the launch traced here: 247 us
  Pallas kernels  205 us (81%)
  local copies, waits for them, and re-layouts  16.5 us (7%)
  between operations  14.3 us (6%)
  starting transfers between devices  8.17 us (3%)
    pallas_call x1, Pallas kernels, experts_apply(): pl.pallas_call(functools.partial(expert_kernel, capacity, sources, shards...  59.3 us
    pallas_call x1, Pallas kernels, shared_gradients(): pl.pallas_call(functools.partial(shared_kernel, chips, planes), out_shape...  47.9 us
    pallas_call x1, Pallas kernels, dispatch(): pl.pallas_call(functools.partial(dispatch_kernel, shards), in_specs=[vmem...  35.6 us
    pallas_call x1, Pallas kernels, backward(): pl.pallas_call(functools.partial(backward_kernel, experts), in_specs=[pl....  33.2 us
    pallas_call x1, Pallas kernels, forward(): pl.pallas_call(functools.partial(forward_kernel, experts), in_specs=[pl.B...  19.1 us
    unnamed x43, local copies, waits for them, and re-layouts  15.7 us
    pallas_call x1, Pallas kernels, route(): pl.pallas_call(functools.partial(route_kernel, experts, capacity), out_sh...  6.28 us
  transfers between devices with their start and end apart: 5, of which 0 were waited for; matrix products, arithmetic and copies ran while one was open for 1% of the time, Pallas kernels for 58%

commit v1 on v0

v1 whole, which is shorter than its diff:
```python
import functools

import jax
import jax.numpy as jnp
from jax import lax
from jax.experimental import pallas as pl
from jax.experimental.pallas import tpu as pltpu
from jax.sharding import PartitionSpec as P

D = 512
HEADS = 8
HEAD = 64
PAIRS = HEADS // 2
PAIR = 2 * HEAD
TOP = 2
SEQ = 1024
TOK_DEV = 1024
LANES = 128
QB = 128
WINDOW = 432
TILE = 256
SLABS = tuple((max(0, QB * (b - 2)), min(SEQ, QB * (b + 3))) for b in range(SEQ // QB))
MIB = 1024 * 1024
MESH = pl.DeviceIdType.MESH

f32 = jnp.float32
bf16 = jnp.bfloat16
NT = (((1,), (1,)), ((), ()))
TN = (((0,), (0,)), ((), ()))


def dot(a, b):
    return jnp.dot(a, b, preferred_element_type=f32)


def dot_nt(a, b):
    return lax.dot_general(a, b, NT, preferred_element_type=f32)


def dot_tn(a, b):
    return lax.dot_general(a, b, TN, preferred_element_type=f32)


def iota(shape, dim):
    return lax.broadcasted_iota(jnp.int32, shape, dim)


def norm_parts(values_in):
    centered = values_in - jnp.mean(values_in, axis=-1, keepdims=True)
    variance = jnp.mean(centered * centered, axis=-1, keepdims=True)
    inverse = lax.rsqrt(variance + 1e-06)
    return (centered * inverse, inverse)


def norm_back(grad_normed, gain, normalized, inverse):
    grad_gain = jnp.sum(grad_normed * normalized, axis=0, keepdims=True)
    scaled = grad_normed * gain
    inner = scaled - jnp.mean(scaled, axis=-1, keepdims=True)
    inner = inner - normalized * jnp.mean(scaled * normalized, axis=-1, keepdims=True)
    return (inner * inverse, grad_gain)


def split2(values_in):
    high = values_in.astype(bf16)
    low = (values_in - high.astype(f32)).astype(bf16)
    return high, low


def row_to_col(row):
    n = row.shape[1]
    return jnp.transpose(jnp.broadcast_to(row, (LANES, n)))[:, :1]


def route_kernel(
    experts,
    capacity,
    picks,
    ranks,
    cot,
    tok,
    gain_attn,
    w_qkv,
    slot_col,
    slot_row,
    counts,
    gz_out,
    normed_out,
    packed_out,
    gz_send,
    normed_attn,
    packed,
    gz_sem,
    sems,
):
    tokens = ranks.shape[1]
    padded = gz_send.shape[1]
    rank_row = ranks[...].astype(f32)
    rank_col = row_to_col(rank_row)
    lane = iota((tokens, LANES), 1)
    pick0 = picks[:, 0:1]
    pick1 = picks[:, 1:2]
    hot = jnp.where(lane == jnp.where(lane < experts, pick0, pick1 + experts), 1.0, 0.0).astype(f32)
    before = (rank_row < rank_col).astype(f32).astype(bf16)
    earlier = dot(before, hot.astype(bf16))
    total = jnp.sum(hot, axis=0, keepdims=True)
    total = jnp.broadcast_to(total, (8, LANES))
    lane8 = iota((8, LANES), 1)
    first = jnp.where(lane8 < experts, total, 0.0)
    earlier = earlier + pltpu.roll(first, experts, axis=1)[:1]
    kept = (hot > 0.5) & (earlier < float(capacity))
    slots = jnp.where(kept, earlier, -1.0)
    slot_col[...] = slots
    slots = jnp.maximum(slots, pltpu.roll(slots, LANES - experts, axis=1))
    slots = jnp.where(lane < experts, slots, -1.0)
    slot_row[...] = jnp.transpose(slots)[:experts]
    kept_lane = jnp.sum(jnp.where(slots >= 0.0, 1.0, 0.0), axis=0, keepdims=True)
    both = total + pltpu.roll(total, LANES - experts, axis=1)
    both = jnp.where(lane8 < experts, both, 0.0)
    sub8 = iota((8, LANES), 0)
    counts[...] = jnp.where(sub8 == 0, kept_lane, jnp.where(sub8 == 1, both, 0.0))

    @pl.loop(0, experts)
    def _(e):
        chosen = iota((padded, tokens), 0).astype(f32) == slot_row[pl.ds(e, 1), :]
        gz_send[e] = dot(chosen.astype(f32).astype(bf16), cot[...]).astype(bf16)
        pltpu.make_async_copy(gz_send.at[e], gz_out.at[e], gz_sem.at[e]).start()

    def stores(i):
        rows = pl.ds(pl.multiple_of(i * TILE, TILE), TILE)
        return (
            pltpu.make_async_copy(normed_attn.at[rows], normed_out.at[rows], sems.at[0, i]),
            pltpu.make_async_copy(packed.at[rows], packed_out.at[rows], sems.at[1, i]),
        )

    @pl.loop(0, tokens // TILE)
    def _(i):
        rows = pl.ds(pl.multiple_of(i * TILE, TILE), TILE)
        normal, unused = norm_parts(tok[rows, :].astype(f32))
        normed = (normal * gain_attn[...]).astype(bf16)
        normed_attn[rows, :] = normed
        packed[rows, :] = dot(normed, w_qkv[...]).astype(bf16)
        for store in stores(i):
            store.start()

    @pl.loop(0, experts)
    def _(e):
        pltpu.make_async_copy(gz_send.at[e], gz_out.at[e], gz_sem.at[e]).wait()

    @pl.loop(0, tokens // TILE)
    def _(i):
        for store in stores(i):
            store.wait()


def route(picks, ranks, cot, tok, gain_attn, w_qkv, experts, capacity, padded):
    tokens = picks.shape[0]
    vmem = pl.BlockSpec(memory_space=pltpu.VMEM)
    anywhere = pl.BlockSpec(memory_space=pl.ANY)
    return pl.pallas_call(
        functools.partial(route_kernel, experts, capacity),
        out_shape=(
            jax.ShapeDtypeStruct((tokens, LANES), f32),
            jax.ShapeDtypeStruct((experts, tokens), f32),
            jax.ShapeDtypeStruct((8, LANES), f32),
            jax.ShapeDtypeStruct((experts, padded, D), bf16),
            jax.ShapeDtypeStruct((tokens, D), bf16),
            jax.ShapeDtypeStruct((tokens, 3 * D), bf16),
        ),
        out_specs=(vmem, vmem, vmem, anywhere, anywhere, anywhere),
        scratch_shapes=[
            pltpu.VMEM((experts, padded, D), bf16),
            pltpu.VMEM((tokens, D), bf16),
            pltpu.VMEM((tokens, 3 * D), bf16),
            pltpu.SemaphoreType.DMA((experts,)),
            pltpu.SemaphoreType.DMA((2, tokens // TILE)),
        ],
        compiler_params=pltpu.CompilerParams(vmem_limit_bytes=40 * MIB),
        cost_estimate=pl.CostEstimate(
            flops=2 * experts * padded * tokens * D, bytes_accessed=6 * MIB, transcendentals=0
        ),
        name="route",
    )(picks, ranks, cot, tok, gain_attn, w_qkv)


def stack_heads(block):
    lane = iota(block.shape, 1)
    zero = jnp.zeros_like(block)
    return jnp.concatenate(
        [jnp.where(lane < HEAD, block, zero), jnp.where(lane < HEAD, zero, block)], axis=0
    )


def unstack_cols(stacked):
    row = iota((PAIR, QB), 0)
    picked = jnp.where(row < HEAD, stacked[:, :QB], stacked[:, QB:])
    return jnp.transpose(picked)


def window_bias(seg_col, seg_row, low, width, query):
    same = seg_col[pl.ds(low, width), :] == seg_row[:, pl.ds(query, QB)]
    half = jnp.where(same, 0.0, -1e30).astype(f32)
    return jnp.concatenate([half, half], axis=1)


def by_window(windows, block, body):
    low = windows[block]
    fits = windows[block + SEQ // QB]

    @pl.when(fits == 1)
    def _():
        body(pl.multiple_of(low, 16), WINDOW)

    @pl.when(fits != 1)
    def _():
        body(0, SEQ)


def forward_kernel(
    experts,
    windows,
    tok,
    seg,
    packed,
    w_proj,
    gain_moe,
    w_router,
    context_out,
    lse,
    residual_out,
    normed_moe_out,
    gates_out,
    gate_row,
    context,
    residual,
    normed_moe,
    gates,
    seg_col,
    seg_row,
    router,
    sems,
):
    writes = [
        pltpu.make_async_copy(source, target, sems.at[i])
        for i, (source, target) in enumerate(
            (
                (context, context_out),
                (residual, residual_out),
                (normed_moe, normed_moe_out),
                (gates, gates_out),
            )
        )
    ]
    tokens = tok.shape[0]
    seg_row[...] = seg[...].astype(f32)
    seg_col[...] = jnp.transpose(jnp.broadcast_to(seg_row[...], (LANES, tokens)))
    router[...] = jnp.zeros_like(router)
    router[:, :experts] = w_router[...]

    @pl.loop(0, tokens // QB)
    def _(block):
        query = pl.multiple_of(block * QB, QB)

        def body(low, width):
            bias = window_bias(seg_col, seg_row, low, width, query)
            spans = [slice(pair * PAIR, (pair + 1) * PAIR) for pair in range(PAIRS)]
            scores = []
            for span in spans:
                q = stack_heads(packed[pl.ds(query, QB), span]) * HEAD ** (-0.5)
                k = packed[pl.ds(low, width), D + span.start : D + span.stop]
                scores.append(dot_nt(k, q.astype(bf16)) + bias)
            peaks = [jnp.max(score, axis=0, keepdims=True) for score in scores]
            exponents = [jnp.exp(score - peak) for score, peak in zip(scores, peaks)]
            totals = [jnp.sum(exponent, axis=0, keepdims=True) for exponent in exponents]
            probs = [(exponent * (1.0 / total)).astype(bf16) for exponent, total in zip(exponents, totals)]
            for pair, span in enumerate(spans):
                lse[pl.ds(block, 1), pair, :] = peaks[pair] + jnp.log(totals[pair])
                v = packed[pl.ds(low, width), 2 * D + span.start : 2 * D + span.stop]
                mixed = dot_tn(v, probs[pair])
                context[pl.ds(query, QB), span] = unstack_cols(mixed).astype(bf16)

        by_window(windows, block, body)

    writes[0].start()

    @pl.loop(0, tokens // TILE)
    def _(i):
        rows = pl.ds(pl.multiple_of(i * TILE, TILE), TILE)
        rest = tok[rows, :].astype(f32) + dot(context[rows, :], w_proj[...])
        residual[rows, :] = rest
        normal, unused = norm_parts(rest)
        normed = (normal * gain_moe[...]).astype(bf16)
        normed_moe[rows, :] = normed
        logits = dot(normed, router[...])
        logits = jnp.where(iota(logits.shape, 1) < experts, logits, -1e30)
        exponent = jnp.exp(logits - jnp.max(logits, axis=1, keepdims=True))
        gates[rows, :] = exponent / jnp.sum(exponent, axis=1, keepdims=True)

    for write in writes[1:]:
        write.start()
    gate_row[...] = jnp.transpose(gates[...])[:experts]
    for write in writes:
        write.wait()


def forward(windows, tok, seg, packed, w_proj, gain_moe, w_router):
    tokens = tok.shape[0]
    experts = w_router.shape[1]
    vmem = pl.BlockSpec(memory_space=pltpu.VMEM)
    anywhere = pl.BlockSpec(memory_space=pl.ANY)
    return pl.pallas_call(
        functools.partial(forward_kernel, experts),
        in_specs=[pl.BlockSpec(memory_space=pltpu.SMEM)] + [vmem] * 6,
        out_specs=[anywhere, vmem] + [anywhere] * 3 + [vmem],
        out_shape=(
            jax.ShapeDtypeStruct((tokens, D), bf16),
            jax.ShapeDtypeStruct((tokens // QB, PAIRS, 2 * QB), f32),
            jax.ShapeDtypeStruct((tokens, D), f32),
            jax.ShapeDtypeStruct((tokens, D), bf16),
            jax.ShapeDtypeStruct((tokens, LANES), f32),
            jax.ShapeDtypeStruct((experts, tokens), f32),
        ),
        scratch_shapes=[
            pltpu.VMEM((tokens, D), bf16),
            pltpu.VMEM((tokens, D), f32),
            pltpu.VMEM((tokens, D), bf16),
            pltpu.VMEM((tokens, LANES), f32),
            pltpu.VMEM((tokens, LANES), f32),
            pltpu.VMEM((1, tokens), f32),
            pltpu.VMEM((D, LANES), bf16),
            pltpu.SemaphoreType.DMA((4,)),
        ],
        compiler_params=pltpu.CompilerParams(vmem_limit_bytes=56 * MIB),
        cost_estimate=pl.CostEstimate(
            flops=64 * 1024 * MIB, bytes_accessed=16 * MIB, transcendentals=4 * MIB
        ),
        name="attention_forward",
    )(windows, tok, seg, packed, w_proj, gain_moe, w_router)


def gelu_parts(x):
    density = jnp.exp(-0.5 * (x * x))
    return 0.5 + 0.5 * lax.erf(x * 2.0**-0.5), x * density * 0.3989422804014327


def shifted(index, by, size):
    return lax.rem(index + by, size)


def paired(index, by, size):
    total = 0
    bit = 1
    while bit < size:
        total = total + bit * lax.rem(index // bit + by // bit, 2)
        bit *= 2
    return total


def exchange(src, dst, send, recv, device):
    return pltpu.make_async_remote_copy(
        src_ref=src, dst_ref=dst, send_sem=send, recv_sem=recv, device_id=device, device_id_type=MESH
    )


def greet(barrier, sources):
    me = lax.axis_index("wide")
    line = lax.axis_index("narrow")

    @pl.loop(1, sources)
    def _(j):
        pl.semaphore_signal(barrier, inc=1, device_id=(paired(me, j, sources), line), device_id_type=MESH)


EARLY = 3


def moe_kernel(
    capacity,
    sources,
    shards,
    slot_row,
    gate_row,
    normed_in,
    gz_in,
    w_in0,
    w_out0,
    w_in1,
    w_out1,
    w_in2,
    w_out2,
    returned,
    back,
    ring,
    grads,
    normed_moe,
    w_ins,
    w_outs,
    rows_send,
    rows,
    scaled,
    gate_slot,
    rows_t,
    gz_t,
    act,
    gpre,
    out_sum,
    back_sum,
    out_low,
    back_low,
    ring_out,
    ring_in,
    load_sem,
    row_sem,
    out_sem,
    back_sem,
    own_sem,
    weight_sem,
    ring_sem,
):
    padded = rows.shape[1]
    tokens = normed_in.shape[0]
    me = lax.axis_index("wide")
    line = lax.axis_index("narrow")
    right = (me, shifted(line, 1, shards))
    left = (me, shifted(line, shards - 1, shards))
    early = ((w_in0, w_out0), (w_in1, w_out1), (w_in2, w_out2))
    loads = [
        pltpu.make_async_copy(normed_in, normed_moe, load_sem.at[0]),
        pltpu.make_async_copy(gz_in, scaled, load_sem.at[1]),
    ]
    for c, pair in reversed(list(enumerate(early))):
        for i, (source, target) in enumerate(zip(pair, (w_ins, w_outs))):
            loads.append(pltpu.make_async_copy(source, target.at[c], load_sem.at[2 + 2 * c + i]))
    for load in loads:
        load.start()
    barrier = pltpu.get_barrier_semaphore()
    greet(barrier, sources)
    for near in (left, right):
        pl.semaphore_signal(barrier, inc=1, device_id=near, device_id_type=MESH)
    gate_slot[...] = jnp.zeros_like(gate_slot)

    def weights_on(c):
        return [
            exchange(part.at[c - 1], part.at[c], weight_sem.at[0, i, c], weight_sem.at[1, i, c], right)
            for i, part in enumerate((w_ins, w_outs))
        ]

    def row_copy(j):
        to = paired(me, j, sources)
        return exchange(rows_send.at[to], rows.at[me], row_sem.at[0, j], row_sem.at[1, j], (to, line))

    def result_copies(j):
        to = paired(me, j, sources)
        return [
            exchange(low.at[to], target.at[me], sem.at[0, j], sem.at[1, j], (to, line))
            for low, target, sem in ((out_low, returned, out_sem), (back_low, back, back_sem))
        ]

    keep = [
        pltpu.make_async_copy(low.at[me], target.at[me], own_sem.at[i])
        for i, (low, target) in enumerate(((out_low, returned), (back_low, back)))
    ]

    for load in loads[:1] + loads[2:4]:
        load.wait()

    @pl.loop(0, sources)
    def _(i):
        j = paired(i, sources - 2, sources)
        e = paired(me, j, sources)
        chosen = iota((padded, tokens), 0).astype(f32) == slot_row[pl.ds(e, 1), :]
        chosen = chosen.astype(f32).astype(bf16)
        rows_send[e] = dot(chosen, normed_moe[...]).astype(bf16)
        gate = gate_row[pl.ds(e, 1), :]
        high, middle = split2(gate)
        low = (gate - high.astype(f32) - middle.astype(f32)).astype(bf16)
        three = jnp.concatenate(
            [high.astype(f32), middle.astype(f32), low.astype(f32), jnp.zeros((5, tokens), f32)], axis=0
        )
        gate_slot[:, :padded] = dot_nt(three.astype(bf16), chosen)
        tail = rows_send[e, padded - 16 :, :].astype(f32)
        sub = iota(tail.shape, 0)
        for part in range(3):
            tail = jnp.where(sub == 13 + part, gate_slot[part : part + 1, :], tail)
        rows_send[e, padded - 16 :, :] = tail.astype(bf16)

        @pl.when(i == 0)
        def _():
            pl.semaphore_wait(barrier, sources + 1)
            for copy in weights_on(EARLY):
                copy.start()

        @pl.when(j != 0)
        def _():
            row_copy(j).start()

    rows[me] = rows_send[me]
    for load in loads[1:2] + loads[4:]:
        load.wait()

    def partner(i):
        return lax.rem(sources - i // 2 * 2, sources) + lax.rem(i, 2)

    def prepare(j):
        s = paired(me, j, sources)

        @pl.when(j != 0)
        def _():
            row_copy(j).wait_recv()

        tail = rows[s, padded - 16 :, :].astype(f32)
        gate = tail[13:14] + tail[14:15] + tail[15:16]
        gate = jnp.transpose(jnp.broadcast_to(gate, (LANES, D)))[:padded, :1]
        live = iota((padded, 1), 0) < capacity
        scaled[s] = (jnp.where(live, gate, 0.0) * scaled[s].astype(f32)).astype(bf16)
        live16 = iota((16, 1), 0) < 16 - (padded - capacity)
        rows[s, padded - 16 :, :] = jnp.where(live16, tail, 0.0).astype(bf16)

    def shard_results(s, c):
        span = pl.ds(pl.multiple_of(s * padded, 16), padded)
        pre = dot(rows[s], w_ins[c])
        phi, slope = gelu_parts(pre)
        act_low = (pre * phi).astype(bf16)
        act[c, span, :] = act_low
        grad_pre = (dot_nt(scaled[s], w_outs[c]) * (phi + slope)).astype(bf16)
        gpre[c, span, :] = grad_pre
        return dot(act_low, w_outs[c]), dot_nt(grad_pre, w_ins[c])

    def send(j, result, grad_rows):
        s = paired(me, j, sources)
        out_low[s] = result.astype(bf16)
        back_low[s] = grad_rows.astype(bf16)

        @pl.when(j != 0)
        def _():
            for copy in result_copies(j):
                copy.start()

        @pl.when(j == 0)
        def _():
            for copy in keep:
                copy.start()

    def run(s, first, last, spot, carried):
        for c in range(first, last):
            result, grad_rows = shard_results(s, c)
            if c > first or carried:
                result = result + out_sum[spot]
                grad_rows = grad_rows + back_sum[spot]
            if c < last - 1 or last < shards:
                out_sum[spot] = result
                back_sum[spot] = grad_rows
        return result, grad_rows

    half = sources // 2

    @pl.loop(0, half)
    def _(i):
        j = partner(i)
        prepare(j)
        run(paired(me, j, sources), 0, EARLY, i, False)

    for c in range(EARLY, shards):
        for copy in weights_on(c):
            copy.wait()
        if c + 1 < shards:
            for copy in weights_on(c + 1):
                copy.start()

    @pl.loop(0, half)
    def _(i):
        j = partner(i)
        send(j, *run(paired(me, j, sources), EARLY, shards, i, True))

    @pl.loop(half, sources)
    def _(i):
        j = partner(i)
        prepare(j)
        send(j, *run(paired(me, j, sources), 0, shards, 0, False))

    for s in range(sources):
        rows_t[:, s * padded : (s + 1) * padded] = jnp.transpose(rows[s])
        gz_t[:, s * padded : (s + 1) * padded] = jnp.transpose(scaled[s])

    def weight_grads(c):
        return dot(rows_t[...], gpre[c]).astype(bf16), dot(gz_t[...], act[c]).astype(bf16)

    ring_out[:D, :], ring_out[D:, :] = weight_grads(1)
    step = exchange(ring_out, ring_in, ring_sem.at[0], ring_sem.at[1], right)
    step.start()
    for c in range(3, shards):
        grads[c - 2, :D, :], grads[c - 2, D:, :] = weight_grads(c)
    grads[0, :D, :], grads[0, D:, :] = weight_grads(0)
    second = weight_grads(2)
    for copy in keep:
        copy.wait()
    step.wait()
    for part in range(2):
        span = slice(part * D, part * D + D)
        ring[span, :] = (ring_in[span, :].astype(f32) + second[part].astype(f32)).astype(bf16)

    @pl.loop(1, sources)
    def _(j):
        row_copy(j).wait_send()
        for copy in result_copies(j):
            copy.wait()


def moe(slot_row, gate_row, normed_moe, gz, early, shards, capacity):
    sources, padded, unused = gz.shape
    tokens = normed_moe.shape[0]
    hidden = early[0][0].shape[1]
    total = sources * padded
    vmem = pl.BlockSpec(memory_space=pltpu.VMEM)
    anywhere = pl.BlockSpec(memory_space=pl.ANY)
    dma = pltpu.SemaphoreType.DMA
    return pl.pallas_call(
        functools.partial(moe_kernel, capacity, sources, shards),
        in_specs=[vmem] * 2 + [anywhere] * (2 + 2 * EARLY),
        out_specs=(anywhere, anywhere, vmem, vmem),
        out_shape=(
            jax.ShapeDtypeStruct(gz.shape, bf16),
            jax.ShapeDtypeStruct(gz.shape, bf16),
            jax.ShapeDtypeStruct((2 * D, hidden), bf16),
            jax.ShapeDtypeStruct((shards - 2, 2 * D, hidden), bf16),
        ),
        scratch_shapes=[
            pltpu.VMEM((tokens, D), bf16),
            pltpu.VMEM((shards, D, hidden), bf16),
            pltpu.VMEM((shards, hidden, D), bf16),
            pltpu.VMEM(gz.shape, bf16),
            pltpu.VMEM(gz.shape, bf16),
            pltpu.VMEM(gz.shape, bf16),
            pltpu.VMEM((8, D), f32),
            pltpu.VMEM((D, total), bf16),
            pltpu.VMEM((D, total), bf16),
            pltpu.VMEM((shards, total, hidden), bf16),
            pltpu.VMEM((shards, total, hidden), bf16),
            pltpu.VMEM((sources // 2, padded, D), f32),
            pltpu.VMEM((sources // 2, padded, D), f32),
            pltpu.VMEM(gz.shape, bf16),
            pltpu.VMEM(gz.shape, bf16),
            pltpu.VMEM((2 * D, hidden), bf16),
            pltpu.VMEM((2 * D, hidden), bf16),
            dma((2 + 2 * EARLY,)),
            dma((2, sources)),
            dma((2, sources)),
            dma((2, sources)),
            dma((2,)),
            dma((2, 2, shards)),
            dma((2,)),
        ],
        compiler_params=pltpu.CompilerParams(
            vmem_limit_bytes=61 * MIB, collective_id=1, has_side_effects=True
        ),
        cost_estimate=pl.CostEstimate(
            flops=12 * total * D * hidden * shards, bytes_accessed=20 * MIB, transcendentals=0
        ),
        name="moe",
    )(slot_row, gate_row, normed_moe, gz, *[part for pair in early for part in pair])


def combine_kernel(
    experts,
    windows,
    seg,
    w_proj,
    gain_moe,
    w_router,
    slot_col,
    cot,
    packed_in,
    context_in,
    lse,
    residual,
    normed_moe,
    gates,
    returned,
    back,
    counts,
    mixed_out,
    grad_residual_out,
    extra_out,
    grad_context,
    grad_proj,
    small,
    pair_grads,
    packed,
    context,
    mixed,
    grad_residual,
    extra,
    hot,
    seg_col,
    seg_row,
    router,
    grad_attn,
    grad_logits,
    grad_k,
    grad_v,
    bias,
    pair_k,
    pair_v,
    sems,
):
    tokens = cot.shape[0]
    slots_all, padded = returned.shape[0] * returned.shape[1], returned.shape[1]
    reads = (
        pltpu.make_async_copy(packed_in, packed, sems.at[0]),
        pltpu.make_async_copy(context_in, context, sems.at[1]),
    )
    writes = (
        pltpu.make_async_copy(mixed, mixed_out, sems.at[2]),
        pltpu.make_async_copy(grad_residual, grad_residual_out, sems.at[3]),
        pltpu.make_async_copy(extra, extra_out, sems.at[4]),
    )
    for read in reads:
        read.start()
    extra[...] = jnp.zeros_like(extra)
    seg_row[...] = seg[...].astype(f32)
    seg_col[...] = jnp.transpose(jnp.broadcast_to(seg_row[...], (LANES, tokens)))
    router[...] = jnp.zeros_like(router)
    router[:, :experts] = w_router[...]
    small[...] = jnp.zeros_like(small)
    small[2:4, :LANES] = counts[:2, :]

    @pl.loop(0, tokens // TILE)
    def _(i):
        rows = pl.ds(pl.multiple_of(i * TILE, TILE), TILE)
        grad_z = cot[rows, :].astype(f32)
        probs = gates[rows, :]
        slots = slot_col[rows, :]
        lane = iota((TILE, LANES), 1)
        rest = residual[rows, :]
        twice = probs + pltpu.roll(probs, experts, axis=1)
        place = jnp.where(lane < experts, lane, lane - experts).astype(f32) * float(padded)
        total = rest
        grad_gates = jnp.zeros((TILE, LANES), f32)
        spots = iota((TILE, slots_all), 1).astype(f32)
        picks = []
        for k in range(TOP):
            mine = (slots >= 0.0) & (lane >= k * experts) & (lane < (k + 1) * experts)
            spot = jnp.sum(jnp.where(mine, place + slots + 1.0, 0.0), axis=1, keepdims=True) - 1.0
            hot[k * TILE : (k + 1) * TILE, :] = (spots == spot).astype(f32).astype(bf16)
            picks.append(mine)
        back_total = dot(hot[:TILE, :] + hot[TILE:, :], back[...].reshape(slots_all, D))
        results = dot(hot[...], returned[...].reshape(slots_all, D))
        for k in range(TOP):
            result = results[k * TILE : (k + 1) * TILE]
            total = total + jnp.sum(jnp.where(picks[k], twice, 0.0), axis=1, keepdims=True) * result
            inner = jnp.sum(result * grad_z, axis=1, keepdims=True)
            grad_gates = grad_gates + jnp.where(picks[k], inner, 0.0)
        grad_gates = grad_gates + pltpu.roll(grad_gates, LANES - experts, axis=1)
        grad_gates = jnp.where(lane < experts, grad_gates, 0.0)
        mixed[rows, :] = total.astype(bf16)
        gate_inner = jnp.sum(probs * grad_gates, axis=1, keepdims=True)
        high, low = split2(probs * (grad_gates - gate_inner))
        grad_logits[rows, :LANES] = high
        grad_logits[rows, LANES:] = low
        grad_normed = back_total + dot_nt(high, router[...]) + dot_nt(low, router[...])
        normal, inverse = norm_parts(rest)
        grad_norm, grad_gain = norm_back(grad_normed, gain_moe[...], normal, inverse)
        small[1:2, :] += grad_gain
        grad_rest = grad_z + grad_norm
        grad_residual[rows, :] = grad_rest
        attn = grad_rest.astype(bf16)
        grad_attn[rows, :] = attn
        grad_context[rows, :] = dot_nt(attn, w_proj[...]).astype(bf16)

    for write in writes[:2]:
        write.start()
    reads[1].wait()
    both = dot_tn(normed_moe[...], grad_logits[...])
    both = jnp.transpose(both[:, :LANES] + both[:, LANES:])
    small[8:, :] = both[:experts]
    grad_proj[...] = dot_tn(context[...], grad_attn[...])
    blocks = tokens // QB
    reads[0].wait()

    @pl.when(windows[3 * blocks] != 1)
    def _():
        grad_k[...] = jnp.zeros_like(grad_k)
        grad_v[...] = jnp.zeros_like(grad_v)

        @pl.loop(0, blocks)
        def _(block):
            query = pl.multiple_of(block * QB, QB)

            @pl.when(windows[2 * blocks + block] != 1)
            def _():
                bias = window_bias(seg_col, seg_row, 0, SEQ, query)
                spans = [slice(pair * PAIR, (pair + 1) * PAIR) for pair in range(PAIRS)]
                keys = pl.ds(0, SEQ)
                queries = [
                    (stack_heads(packed[pl.ds(query, QB), span]) * HEAD ** (-0.5)).astype(bf16) for span in spans
                ]
                grads = [stack_heads(grad_context[pl.ds(query, QB), span]) for span in spans]
                probs = []
                grad_probs = []
                for pair, span in enumerate(spans):
                    k = packed[keys, D + span.start : D + span.stop]
                    v = packed[keys, 2 * D + span.start : 2 * D + span.stop]
                    probs.append(jnp.exp(dot_nt(k, queries[pair]) + bias - lse[pl.ds(block, 1), pair, :]))
                    grad_probs.append(dot_nt(v, grads[pair]))
                grad_scores = []
                for pair, span in enumerate(spans):
                    grad_v[keys, span] += dot(probs[pair].astype(bf16), grads[pair])
                    weighted = probs[pair] * grad_probs[pair]
                    inner = jnp.sum(weighted, axis=0, keepdims=True)
                    grad_scores.append((weighted - probs[pair] * inner).astype(bf16))
                for pair, span in enumerate(spans):
                    k = packed[keys, D + span.start : D + span.stop]
                    grad_k[keys, span] += dot(grad_scores[pair], queries[pair])
                    grad_q = unstack_cols(dot_tn(k, grad_scores[pair])) * HEAD ** (-0.5)
                    extra[pl.ds(query, QB), span] = grad_q.astype(bf16)
                grad_context[pl.ds(query, QB), :] = jnp.zeros((QB, D), bf16)

        extra[:, D : 2 * D] = grad_k[...].astype(bf16)
        extra[:, 2 * D :] = grad_v[...].astype(bf16)

    writes[2].start()
    slab_bias(bias, seg_col, seg_row[...])
    pair_backward(0, packed, grad_context, lse, extra, bias, pair_k, pair_v, pair_grads)
    for write in writes:
        write.wait()


def combine(experts, windows, *operands):
    cot = operands[5]
    returned = operands[-3]
    tokens = cot.shape[0]
    vmem = pl.BlockSpec(memory_space=pltpu.VMEM)
    anywhere = pl.BlockSpec(memory_space=pl.ANY)
    return pl.pallas_call(
        functools.partial(combine_kernel, experts),
        in_specs=[pl.BlockSpec(memory_space=pltpu.SMEM)] + [vmem] * 6 + [anywhere] * 2 + [vmem] * (len(operands) - 8),
        out_specs=[anywhere, anywhere, anywhere, vmem, vmem, vmem, vmem],
        out_shape=(
            jax.ShapeDtypeStruct((tokens, D), bf16),
            jax.ShapeDtypeStruct((tokens, D), f32),
            jax.ShapeDtypeStruct((tokens, 3 * D), bf16),
            jax.ShapeDtypeStruct((tokens, D), bf16),
            jax.ShapeDtypeStruct((D, D), f32),
            jax.ShapeDtypeStruct((8 + experts, D), f32),
            jax.ShapeDtypeStruct((tokens, 3 * PAIR), bf16),
        ),
        scratch_shapes=[
            pltpu.VMEM((tokens, 3 * D), bf16),
            pltpu.VMEM((tokens, D), bf16),
            pltpu.VMEM((tokens, D), bf16),
            pltpu.VMEM((tokens, D), f32),
            pltpu.VMEM((tokens, 3 * D), bf16),
            pltpu.VMEM((TOP * TILE, returned.shape[0] * returned.shape[1]), bf16),
            pltpu.VMEM((tokens, LANES), f32),
            pltpu.VMEM((1, tokens), f32),
            pltpu.VMEM((D, LANES), bf16),
            pltpu.VMEM((tokens, D), bf16),
            pltpu.VMEM((tokens, 2 * LANES), bf16),
            pltpu.VMEM((tokens, D), f32),
            pltpu.VMEM((tokens, D), f32),
            pltpu.VMEM((SLAB_AT[-1], QB), f32),
            pltpu.VMEM((tokens, PAIR), f32),
            pltpu.VMEM((tokens, PAIR), f32),
            pltpu.SemaphoreType.DMA((5,)),
        ],
        compiler_params=pltpu.CompilerParams(vmem_limit_bytes=60 * MIB),
        cost_estimate=pl.CostEstimate(
            flops=30 * 1024 * MIB, bytes_accessed=30 * MIB, transcendentals=4 * MIB
        ),
        name="combine",
    )(windows, *operands)


SLAB_AT = tuple(sum(high - low for low, high in SLABS[:b]) for b in range(len(SLABS) + 1))


def slab_bias(bias, seg_col, seg_row):
    for b, (low, high) in enumerate(SLABS):
        same = seg_col[low:high, :] == seg_row[:, b * QB : (b + 1) * QB]
        bias[SLAB_AT[b] : SLAB_AT[b + 1], :] = jnp.where(same, 0.0, -1e30)


def pair_backward(pair, packed, grad_context, lse, extra, bias, grad_k, grad_v, out):
    def span(which):
        return pl.ds(pl.multiple_of(which * D + pair * PAIR, PAIR), PAIR)

    grad_k[...] = extra[:, span(1)].astype(f32)
    grad_v[...] = extra[:, span(2)].astype(f32)
    for group in range(0, len(SLABS), 4):
        blocks = range(group, group + 4)
        queries, grads, probs, grad_probs, grad_scores = [], [], [], [], []
        for b in blocks:
            low, high = SLABS[b]
            rows = slice(b * QB, (b + 1) * QB)
            queries.append((stack_heads(packed[rows, span(0)]) * HEAD ** (-0.5)).astype(bf16))
            grads.append(stack_heads(grad_context[rows, span(0)]))
            masked = bias[SLAB_AT[b] : SLAB_AT[b + 1], :]
            scores = dot_nt(packed[low:high, span(1)], queries[-1]) + jnp.concatenate([masked, masked], axis=1)
            probs.append(jnp.exp(scores - lse[b, pl.ds(pair, 1), :]))
            grad_probs.append(dot_nt(packed[low:high, span(2)], grads[-1]))
        for i, b in enumerate(blocks):
            low, high = SLABS[b]
            grad_v[low:high, :] += dot(probs[i].astype(bf16), grads[i])
            weighted = probs[i] * grad_probs[i]
            inner = jnp.sum(weighted, axis=0, keepdims=True)
            grad_scores.append((weighted - probs[i] * inner).astype(bf16))
        for i, b in enumerate(blocks):
            low, high = SLABS[b]
            rows = slice(b * QB, (b + 1) * QB)
            grad_k[low:high, :] += dot(grad_scores[i], queries[i])
            grad_q = unstack_cols(dot_tn(packed[low:high, span(1)], grad_scores[i])) * HEAD ** (-0.5)
            out[rows, :PAIR] = (grad_q + extra[rows, span(0)].astype(f32)).astype(bf16)
    out[:, PAIR : 2 * PAIR] = grad_k[...].astype(bf16)
    out[:, 2 * PAIR :] = grad_v[...].astype(bf16)


def shared_kernel(
    chips,
    planes,
    seg,
    lse,
    partial,
    gain_attn,
    first_in,
    packed_in,
    grad_context_in,
    extra_in,
    normed_attn_in,
    grad_proj_in,
    w_qkv_in,
    tok_in,
    grad_residual_in,
    summed,
    small,
    grad_tokens_out,
    pair_grads,
    packed,
    grad_context,
    extra,
    normed_attn,
    grad_proj,
    w_qkv,
    tok,
    grad_residual,
    grad_tokens,
    normed_t,
    seg_col,
    bias,
    grad_k,
    grad_v,
    grad_packed,
    half,
    core_out,
    core_in,
    chip_out,
    chip_in,
    plane_out,
    plane_in,
    small_own,
    small_core,
    small_chip,
    small_plane,
    load_sem,
    store_sem,
    core_sem,
    chip_sem,
    plane_sem,
    plane_sem2,
    chip_sem2,
    core_sem2,
    small_sem,
    small_chip_sem,
    small_plane_sem,
):
    tokens = tok.shape[0]
    stages = 16 // planes
    pairs = PAIRS // stages
    tiles = tokens // TILE
    wide = lax.axis_index("wide")
    plane = lax.axis_index("narrow")
    core = lax.rem(wide, 2)
    chip = wide // 2
    share = D // (2 * chips)
    partner = (chip * 2 + 1 - core, plane)
    mine = pl.ds(pl.multiple_of(core * (D // 2), D // 2), D // 2)
    other = pl.ds(pl.multiple_of((1 - core) * (D // 2), D // 2), D // 2)
    chunk = pl.ds(pl.multiple_of(core * (D // 2) + chip * share, share), share)
    own_chunk = pl.ds(pl.multiple_of(chip * share, share), share)

    loads = [
        pltpu.make_async_copy(source, target, load_sem.at[i])
        for i, (source, target) in enumerate(
            (
                (first_in, pair_grads),
                (normed_attn_in, normed_attn),
                (grad_proj_in, grad_proj),
                (packed_in, packed),
                (grad_context_in, grad_context),
                (extra_in, extra),
                (w_qkv_in, w_qkv),
                (tok_in, tok),
                (grad_residual_in, grad_residual),
            )
        )
    ]
    for load in loads:
        load.start()

    def chip_at(j):
        to = shifted(chip, j, chips)
        return to, (to * 2 + core, plane)

    def plane_at(j):
        to = shifted(plane, j, planes)
        return to, (wide, to)

    barrier = pltpu.get_barrier_semaphore()
    pl.semaphore_signal(barrier, inc=1, device_id=partner, device_id_type=MESH)

    @pl.loop(1, chips)
    def _(j):
        pl.semaphore_signal(barrier, inc=1, device_id=chip_at(j)[1], device_id_type=MESH)

    @pl.loop(1, planes)
    def _(j):
        pl.semaphore_signal(barrier, inc=1, device_id=plane_at(j)[1], device_id_type=MESH)

    def blocks(stage):
        return pl.ds(stage * planes, planes)

    def core_copy(stage):
        at = blocks(stage)
        return exchange(core_out.at[at], core_in.at[at], core_sem.at[0, stage], core_sem.at[1, stage], partner)

    def chip_copy(stage, j):
        to, device = chip_at(j)
        rows = pl.ds(pl.multiple_of(to * share, share), share)
        at = blocks(stage)
        return exchange(
            chip_out.at[at, rows], chip_in.at[j, at], chip_sem.at[0, stage, j], chip_sem.at[1, stage, j], device
        )

    def plane_copy(stage, j):
        to, device = plane_at(j)
        return exchange(
            plane_out.at[stage * planes + to],
            plane_in.at[j, stage],
            plane_sem.at[0, stage, j],
            plane_sem.at[1, stage, j],
            device,
        )

    def plane_back(stage, j):
        spot = summed.at[stage * planes + plane, chunk]
        return exchange(spot, spot, plane_sem2.at[0, stage, j], plane_sem2.at[1, stage, j], plane_at(j)[1])

    def chip_back(stage, j):
        spot = summed.at[blocks(stage), chunk]
        return exchange(spot, spot, chip_sem2.at[0, stage, j], chip_sem2.at[1, stage, j], chip_at(j)[1])

    def core_back(stage):
        spot = summed.at[blocks(stage), mine]
        return exchange(spot, spot, core_sem2.at[0, stage], core_sem2.at[1, stage], partner)

    def small_core_copy():
        return exchange(small_own, small_core, small_sem.at[0], small_sem.at[1], partner)

    def small_chip_copy(j):
        spot = small_chip.at[chip]
        return exchange(spot, spot, small_chip_sem.at[0, j], small_chip_sem.at[1, j], chip_at(j)[1])

    def small_plane_copy(j):
        spot = small_plane.at[plane]
        return exchange(spot, spot, small_plane_sem.at[0, j], small_plane_sem.at[1, j], plane_at(j)[1])

    def pair_products(pair):
        spare = dot(normed_t[other, :], pair_grads[...])
        own = dot(normed_t[mine, :], pair_grads[...])
        lanes = pl.ds(pl.multiple_of(pair * PAIR, PAIR), PAIR)
        for which in range(3):
            at = slice(which * PAIR, (which + 1) * PAIR)
            core_out[pair * 4 + which] = spare[:, at].astype(bf16)
            half[pair * 4 + which] = own[:, at]
            grad_packed[:, pl.ds(pl.multiple_of(which * D + pair * PAIR, PAIR), PAIR)] = pair_grads[:, at]
        core_out[pair * 4 + 3] = grad_proj[other, lanes].astype(bf16)
        half[pair * 4 + 3] = grad_proj[mine, lanes]

    def chip_stage(stage):
        core_copy(stage).wait_recv()
        at = blocks(stage)
        total = half[at] + core_in[at].astype(f32)
        half[at] = total
        chip_out[at] = total.astype(bf16)

        @pl.loop(1, chips)
        def _(j):
            chip_copy(stage, j).start()

    def plane_stage(stage):
        at = blocks(stage)
        total = half[at, own_chunk, :]
        for j in range(1, chips):
            chip_copy(stage, j).wait_recv()
            total = total + chip_in[j, at].astype(f32)
        half[at, own_chunk, :] = total
        plane_out[at] = total.astype(bf16)

        @pl.loop(1, planes)
        def _(j):
            plane_copy(stage, j).start()

    def own_stage(stage):
        total = half[stage * planes + plane, own_chunk, :]
        for j in range(1, planes):
            plane_copy(stage, j).wait_recv()
            total = total + plane_in[j, stage].astype(f32)
        summed[stage * planes + plane, chunk, :] = total.astype(bf16)

        @pl.loop(1, planes)
        def _(j):
            plane_back(stage, j).start()

    def gather_stage(stage):
        @pl.loop(1, planes)
        def _(j):
            plane_back(stage, j).wait_recv()

        @pl.loop(1, chips)
        def _(j):
            chip_back(stage, j).start()

    def last_stage(stage):
        @pl.loop(1, chips)
        def _(j):
            chip_back(stage, j).wait_recv()

        core_back(stage).start()

    def norm_tile(i):
        rows = slice(i * TILE, (i + 1) * TILE)
        grad_normed = dot_nt(grad_packed[rows, :], w_qkv[...])
        normal, inverse = norm_parts(tok[rows, :].astype(f32))
        grad_norm, grad_gain = norm_back(grad_normed, gain_attn[...], normal, inverse)
        small_own[0:1, :] += grad_gain
        grad_tokens[rows, :] = grad_residual[rows, :] + grad_norm

    small_own[...] = partial[...]
    seg_row = seg[...].astype(f32)
    seg_col[...] = jnp.transpose(jnp.broadcast_to(seg_row, (LANES, tokens)))
    slab_bias(bias, seg_col, seg_row)
    for load in loads[:3]:
        load.wait()
    normed_t[...] = jnp.transpose(normed_attn[...])
    pair_products(0)
    pl.semaphore_wait(barrier, chips + planes - 1)
    if pairs == 1:
        core_copy(0).start()
    for load in loads[3:6]:
        load.wait()

    @pl.loop(1, PAIRS)
    def _(pair):
        pair_backward(pair, packed, grad_context, lse, extra, bias, grad_k, grad_v, pair_grads)
        pair_products(pair)

        @pl.when(lax.rem(pair + 1, pairs) == 0)
        def _():
            stage = pair // pairs
            core_copy(stage).start()

            @pl.when(stage > 0)
            def _():
                chip_stage(stage - 1)

            @pl.when(stage > 1)
            def _():
                plane_stage(stage - 2)

            @pl.when(stage > 2)
            def _():
                own_stage(stage - 3)

    for load in loads[6:]:
        load.wait()
    steps = (chip_stage, plane_stage, own_stage, gather_stage, last_stage)
    for late in range(len(steps)):
        if late == 0:
            norm_tile(0)
        for i, step in enumerate(steps):
            stage = stages - 1 + late - i
            if i >= late and 0 <= stage < stages:
                step(stage)
        if late == 0:
            for i in range(1, tiles):
                norm_tile(i)
            small_core_copy().start()
            store = pltpu.make_async_copy(grad_tokens, grad_tokens_out, store_sem)
            store.start()
        if late == 1:
            small_core_copy().wait_recv()
            small_chip[chip] = small_own[...] + small_core[...]

            @pl.loop(1, chips)
            def _(j):
                small_chip_copy(j).start()

        if late == 2:

            @pl.loop(1, chips)
            def _(j):
                small_chip_copy(j).wait_recv()

            total = small_chip[0]
            for c in range(1, chips):
                total = total + small_chip[c]
            small_plane[plane] = total

            @pl.loop(1, planes)
            def _(j):
                small_plane_copy(j).start()

    @pl.loop(1, planes)
    def _(j):
        small_plane_copy(j).wait_recv()

    total = small_plane[0]
    for c in range(1, planes):
        total = total + small_plane[c]
    small[...] = total
    store.wait()

    @pl.loop(0, stages)
    def _(stage):
        core_back(stage).wait()
        core_copy(stage).wait_send()

        @pl.loop(1, chips)
        def _(j):
            chip_back(stage, j).wait_send()
            chip_copy(stage, j).wait_send()

        @pl.loop(1, planes)
        def _(j):
            plane_back(stage, j).wait_send()
            plane_copy(stage, j).wait_send()

    @pl.loop(1, planes)
    def _(j):
        small_plane_copy(j).wait_send()

    @pl.loop(1, chips)
    def _(j):
        small_chip_copy(j).wait_send()

    small_core_copy().wait_send()


def shared_gradients(*operands):
    partial, packed = operands[2], operands[5]
    tokens = packed.shape[0]
    chips = lax.axis_size("wide") // 2
    planes = lax.axis_size("narrow")
    stages = 16 // planes
    share = D // (2 * chips)
    rows = partial.shape[0]
    dma = pltpu.SemaphoreType.DMA
    vmem = pl.BlockSpec(memory_space=pltpu.VMEM)
    anywhere = pl.BlockSpec(memory_space=pl.ANY)
    return pl.pallas_call(
        functools.partial(shared_kernel, chips, planes),
        in_specs=[vmem] * 4 + [anywhere] * 9,
        out_specs=(vmem, vmem, anywhere),
        out_shape=(
            jax.ShapeDtypeStruct((16, D, LANES), bf16),
            jax.ShapeDtypeStruct((rows, D), f32),
            jax.ShapeDtypeStruct((tokens, D), f32),
        ),
        scratch_shapes=[pltpu.VMEM(operand.shape, operand.dtype) for operand in operands[4:]]
        + [
            pltpu.VMEM((tokens, D), f32),
            pltpu.VMEM((D, tokens), bf16),
            pltpu.VMEM((tokens, LANES), f32),
            pltpu.VMEM((SLAB_AT[-1], QB), f32),
            pltpu.VMEM((tokens, PAIR), f32),
            pltpu.VMEM((tokens, PAIR), f32),
            pltpu.VMEM((tokens, 3 * D), bf16),
            pltpu.VMEM((16, D // 2, LANES), f32),
            pltpu.VMEM((16, D // 2, LANES), bf16),
            pltpu.VMEM((16, D // 2, LANES), bf16),
            pltpu.VMEM((16, D // 2, LANES), bf16),
            pltpu.VMEM((chips, 16, share, LANES), bf16),
            pltpu.VMEM((16, share, LANES), bf16),
            pltpu.VMEM((planes, stages, share, LANES), bf16),
            pltpu.VMEM((rows, D), f32),
            pltpu.VMEM((rows, D), f32),
            pltpu.VMEM((chips, rows, D), f32),
            pltpu.VMEM((planes, rows, D), f32),
            dma((9,)),
            dma,
            dma((2, stages)),
            dma((2, stages, chips)),
            dma((2, stages, planes)),
            dma((2, stages, planes)),
            dma((2, stages, chips)),
            dma((2, stages)),
            dma((2,)),
            dma((2, chips)),
            dma((2, planes)),
        ],
        compiler_params=pltpu.CompilerParams(
            vmem_limit_bytes=58 * MIB, collective_id=2, has_side_effects=True
        ),
        cost_estimate=pl.CostEstimate(
            flops=12 * tokens * D * D, bytes_accessed=16 * MIB, transcendentals=0
        ),
        name="shared_gradients",
    )(*operands)


def finish_kernel(experts, summed, ring, own, small, tokens_in, qkv, proj, grad_in, grad_out, rest, router, tokens_out, sem):
    copy = pltpu.make_async_copy(tokens_in, tokens_out, sem)
    copy.start()
    for n in range(16):
        pair, which = divmod(n, 4)
        lanes = slice(pair * PAIR, (pair + 1) * PAIR)
        if which < 3:
            qkv[:, which * D + lanes.start : which * D + lanes.stop] = summed[n].astype(f32)
        else:
            proj[:, lanes] = summed[n].astype(f32)
    total = ring[...].astype(f32) + own[...].astype(f32)
    grad_in[0] = total[:D, :]
    grad_out[0] = jnp.transpose(total[D:, :])
    rest[...] = small[:8, :]
    router[...] = jnp.transpose(jnp.concatenate([small[8:, :], jnp.zeros((LANES - experts, D), f32)], axis=0))[
        :, :experts
    ]
    copy.wait()


def finish(experts, summed, ring, own, small, tokens_in):
    hidden = own.shape[1]
    vmem = pl.BlockSpec(memory_space=pltpu.VMEM)
    anywhere = pl.BlockSpec(memory_space=pl.ANY)
    return pl.pallas_call(
        functools.partial(finish_kernel, experts),
        in_specs=[vmem, vmem, vmem, vmem, anywhere],
        out_specs=[vmem] * 6 + [anywhere],
        out_shape=(
            jax.ShapeDtypeStruct((D, 3 * D), f32),
            jax.ShapeDtypeStruct((D, D), f32),
            jax.ShapeDtypeStruct((1, D, hidden), f32),
            jax.ShapeDtypeStruct((1, hidden, D), f32),
            jax.ShapeDtypeStruct((8, D), f32),
            jax.ShapeDtypeStruct((D, experts), f32),
            jax.ShapeDtypeStruct(tokens_in.shape, f32),
        ),
        scratch_shapes=[pltpu.SemaphoreType.DMA],
        compiler_params=pltpu.CompilerParams(vmem_limit_bytes=40 * MIB),
        cost_estimate=pl.CostEstimate(flops=0, bytes_accessed=14 * MIB, transcendentals=0),
        name="finish",
    )(summed, ring, own, small, tokens_in)


def per_device(
    tokens,
    segment_ids,
    expert_picks,
    priority_ranks,
    gain_attn,
    w_qkv,
    w_proj,
    gain_moe,
    w_router,
    w_in,
    w_out,
    cotangent,
):
    experts = w_router.shape[1]
    capacity = (21 * TOP * TOK_DEV + 20 * experts - 1) // (20 * experts)
    padded = (capacity + 3 + 15) // 16 * 16
    gain_attn = gain_attn.reshape(1, D)
    gain_moe = gain_moe.reshape(1, D)
    seg = segment_ids.reshape(1, SEQ)
    first = jnp.sum((segment_ids[None, :] < segment_ids[0::QB, None]).astype(jnp.int32), axis=1)
    after = jnp.sum((segment_ids[None, :] <= segment_ids[QB - 1 :: QB, None]).astype(jnp.int32), axis=1)
    low = jnp.minimum(first // 16 * 16, SEQ - WINDOW)
    fits = (after - low <= WINDOW).astype(jnp.int32)
    slab_low = jnp.array([slab[0] for slab in SLABS], jnp.int32)
    slab_high = jnp.array([slab[1] for slab in SLABS], jnp.int32)
    slab_fits = ((first >= slab_low) & (after <= slab_high)).astype(jnp.int32)
    windows = jnp.concatenate([low, fits, slab_fits, jnp.min(slab_fits, keepdims=True)])

    line = lax.axis_size("narrow")
    ring_steps = [(i, (i + 1) % line) for i in range(line)]
    together = lax.optimization_barrier

    def pass_on(values):
        return lax.ppermute(values, "narrow", ring_steps)

    early = [(w_in[0], w_out[0])]
    early.append(pass_on(early[0]))
    slot_col, slot_row, counts, gz_send, normed_attn, packed = route(
        expert_picks, priority_ranks, cotangent, tokens, gain_attn, w_qkv, experts, capacity, padded
    )
    gz = lax.all_to_all(gz_send, "wide", split_axis=0, concat_axis=0, tiled=True)
    early.append(pass_on(together((early[1], slot_row))[0]))
    context, lse, residual, normed_moe, gates, gate_row = forward(
        windows, tokens, seg, packed, w_proj, gain_moe, w_router
    )
    returned, back, ring, grads = moe(slot_row, gate_row, normed_moe, gz, early, line, capacity)
    ring = pass_on(ring)
    mixed, grad_residual, extra, grad_context, grad_proj, partial, first_pair = combine(
        experts,
        windows,
        seg,
        w_proj,
        gain_moe,
        w_router,
        slot_col,
        cotangent,
        packed,
        context,
        lse,
        residual,
        normed_moe,
        gates,
        returned,
        back,
        counts,
    )
    ring, grad_context = together((ring, grad_context))
    for k in range(1, line - 2):
        ring = pass_on((ring.astype(f32) + grads[k].astype(f32)).astype(bf16))
    summed, small, grad_tokens = shared_gradients(
        seg,
        lse,
        partial,
        gain_attn,
        first_pair,
        packed,
        grad_context,
        extra,
        normed_attn,
        grad_proj,
        w_qkv,
        tokens,
        grad_residual,
    )
    grad_qkv, grad_proj, grad_in, grad_out, rest, grad_router, grad_tokens = finish(
        experts, summed, ring, grads[0], small, grad_tokens
    )
    counted = rest[2:4, :experts].astype(jnp.int32)
    return (
        mixed,
        grad_tokens,
        rest[0],
        grad_qkv,
        grad_proj,
        rest[1],
        grad_router,
        grad_in,
        grad_out,
        counted[0],
        counted[1] - counted[0],
    )


def solution(mesh):
    both = ("wide", "narrow")
    placed = (
        P(both, None),
        P(both),
        P(both, None),
        P(both, None),
        P(),
        P(),
        P(),
        P(),
        P(),
        P("wide", None, "narrow"),
        P("wide", "narrow", None),
        P(both, None),
    )
    return jax.shard_map(
        per_device,
        mesh=mesh,
        in_specs=placed,
        out_specs=(
            P(both, None),
            P(both, None),
            P(),
            P(),
            P(),
            P(),
            P(),
            P("wide", None, "narrow"),
            P("wide", "narrow", None),
            P(),
            P(),
        ),
        check_vma=False,
    )
```

time: 252 us -> 235 us (0.933)
  Pallas kernels: 205 us -> 184 us
  between operations: 14.3 us -> 1.09 us
  waiting for transfers between devices: 0.69 us -> 9.92 us
  starting transfers between devices: 8.17 us -> 12.4 us
  local copies, waits for them, and re-layouts: 16.5 us -> 19.3 us
    pallas_call x4 -> x3, Pallas kernels: 176 us -> 155 us  [the longest x1 81.6 us: moe(): pl.pallas_call(functools.partial(moe_kernel, capacity, sources, shards),...]
    ppermute x3 -> x6, waiting for transfers between devices: 0.01 us -> 9.91 us  [pass_on(): return lax.ppermute(values, 'narrow', ring_steps)]
    ppermute x3 -> x6, starting transfers between devices: 4.27 us -> 8.59 us  [pass_on(): return lax.ppermute(values, 'narrow', ring_steps)]
    unnamed x43 -> x45, local copies, waits for them, and re-layouts: 15.7 us -> 18.4 us
    pallas_call x1, Pallas kernels: 19.1 us -> 16.4 us  [forward(): pl.pallas_call(functools.partial(forward_kernel, experts), in_specs=[pl.B...]
  transfers between devices with their start and end apart: 5 -> 7, of which waited for: 0 -> 2; matrix products, arithmetic and copies ran while one was open for 1% -> 2% of each run, Pallas kernels for 58% -> 43%
where the time goes in v1:
time: 235 us; the launch traced here: 231 us
  Pallas kernels  184 us (78%)
  local copies, waits for them, and re-layouts  19.3 us (8%)
  starting transfers between devices  12.4 us (5%)
  waiting for transfers between devices  9.92 us (4%)
  other arithmetic  3.88 us (2%)
    pallas_call x1, Pallas kernels, moe(): pl.pallas_call(functools.partial(moe_kernel, capacity, sources, shards),...  81.6 us
    pallas_call x1, Pallas kernels, shared_gradients(): pl.pallas_call(functools.partial(shared_kernel, chips, planes), in_specs=...  49.9 us
    pallas_call x1, Pallas kernels, combine(): pl.pallas_call(functools.partial(combine_kernel, experts), in_specs=[pl.B...  23.7 us
    unnamed x45, local copies, waits for them, and re-layouts  18.4 us
    pallas_call x1, Pallas kernels, forward(): pl.pallas_call(functools.partial(forward_kernel, experts), in_specs=[pl.B...  16.4 us
    ppermute x6, waiting for transfers between devices, pass_on(): return lax.ppermute(values, 'narrow', ring_steps)  9.91 us
    pallas_call x1, Pallas kernels, route(): pl.pallas_call(functools.partial(route_kernel, experts, capacity), out_sh...  8.59 us
    ppermute x6, starting transfers between devices, pass_on(): return lax.ppermute(values, 'narrow', ring_steps)  8.59 us
  transfers between devices with their start and end apart: 7, of which 2 were waited for; matrix products, arithmetic and copies ran while one was open for 2% of the time, Pallas kernels for 43%

profile of v1, /device:TPU:0, one launch (start us, length us, event | category | flops | bytes accessed | tf_op | source)
XLA Modules:
  0.0 231.1 jit_solution(14892487046009697179)
XLA Ops:
  0.6 3.1 %collective-permute-start = (bf16[512,512]{1,0:T(8,128)(2,1)}, bf16[512,512]{1,0:T(8,128)(2,1)S(1)}, u32[]{:S(2)}, u32[]{:S(2)}) collective-permute-start(bf16[512,512]{1,0:T(8,128)(2,1)} %bitcast.25), channel_id=1, source_target_pairs={{0,1},{1,2},{2,3},{3,0},{4,5},{5,6},{6,7},{7,4},{8,9},{9,10},{10,1... | collective-permute-start | bytes 1572872 | tf_op jit(solution)/shard_map/ppermute | solution.py:1397
  3.7 1.6 collective-permute-start.1
  5.3 0.9 copy.29.picks
  6.2 1.4 copy-done.3
  7.6 1.2 copy-done.4
  8.9 0.7 copy-done.7
  9.5 1.2 copy-done.8
  10.8 0.7 copy-done.9
  11.4 8.6 %route.1 = (f32[1024,128]{1,0:T(8,128)S(1)}, f32[8,1024]{1,0:T(8,128)S(1)}, f32[8,128]{1,0:T(8,128)S(1)}, bf16[8,272,512]{2,1,0:T(8,128)(2,1)}, bf16[1024,512]{1...) custom-call(s32[1024,2]{1,0:T(8,128)S(1)} %copy.29.picks, s32[1,1024]{1,0:T(1,128)S(1)} %copy-done.9, ...), custom_call_target="tpu_custom_call" | custom-call | flops 2281701376 | bytes 6291456 | tf_op jit(solution)/shard_map/route/pallas_call | solution.py:159
  20.1 1.7 copy-done
  21.7 1.0 copy-done.5
  22.7 0.8 copy-done.10
  24.7 3.9 %all-to-all-start = ((bf16[8,272,512]{2,1,0:T(8,128)(2,1)}), bf16[8,272,512]{2,1,0:T(8,128)(2,1)S(1)}, u32[]{:S(2)}, u32[]{:S(2)}) async-start(bf16[8,272,512]{2,1,0:T(8,128)(2,1)} %get-tuple-element.57), calls=%async_computation | async-start | bytes 4456448 | tf_op jit(solution)/shard_map/all_to_all | solution.py:1404
  28.8 0.8 copy.31.w_router
  30.5 1.2 pad_add_fusion.windows
  31.7 1.6 collective-permute-start.2
  33.4 0.7 collective-permute-start.3
  34.1 16.4 %attention_forward.1 = (bf16[1024,512]{1,0:T(8,128)(2,1)}, f32[8,4,256]{2,1,0:T(4,128)}, f32[1024,512]{1,0:T(8,128)}, bf16[1024,512]{1,0:T(8,128)(2,1)}, f32[1024,128]{1,0:T(8,128)}, /*index=5*/f32[8,1024]{1,0:T(8,128)}) custom-call(s32[25]{0:T(128)} %pad_add_fusion.windows, bf16[1024,512]{1,0:T(8,128)(2,1)} %tok_in.1, s32[1,1024]{1,0:T(1,128)} %bitcast.20, ...), custom_call_target="tpu_custom_call" | custom-call | flops 68719476736 | bytes 16777216 | tf_op jit(solution)/shard_map/attention_forward/pallas_call | solution.py:310
  50.6 0.8 copy-done.20
  51.4 7.9 %collective-permute-done.3.w_out2 = bf16[512,512]{1,0:T(8,128)(2,1)} collective-permute-done((bf16[512,512]{1,0:T(8,128)(2,1)}, bf16[512,512]{1,0:T(8,128)(2,1)}, u32[]{:S(2)}, u32[]{:S(2)}) %collective-permute-start.3) | collective-permute-done | bytes 524320 | tf_op jit(solution)/shard_map/ppermute | solution.py:1397
  59.3 1.4 copy-done.13
  60.7 81.6 %moe.1 = (bf16[8,272,512]{2,1,0:T(8,128)(2,1)}, bf16[8,272,512]{2,1,0:T(8,128)(2,1)}, bf16[1024,512]{1,0:T(8,128)(2,1)}, bf16[2,1024,512]{2,1,0:T(8,128)(2,1)}) custom-call(f32[8,1024]{1,0:T(8,128)} %copy-done.11, f32[8,1024]{1,0:T(8,128)} %get-tuple-element.56.gate_row, bf16[1024,512]{1,0:T(8,128)(2,1)} %get-tuple-element.53.normed_in.normed_moe, ...), custom_call_target="tpu_custom_call" | custom-call | flops 27380416512 | bytes 20971520 | tf_op jit(solution)/shard_map/moe/pallas_call | solution.py:616
  142.3 1.6 collective-permute-start.4
  143.8 23.7 %combine.1 = (bf16[1024,512]{1,0:T(8,128)(2,1)}, f32[1024,512]{1,0:T(8,128)}, bf16[1024,1536]{1,0:T(8,128)(2,1)}, bf16[1024,512]{1,0:T(8,128)(2,1)}, f32[512,512...) custom-call(s32[25]{0:T(128)} %pad_add_fusion.windows, s32[1,1024]{1,0:T(1,128)} %bitcast.21, ...), custom_call_target="tpu_custom_call" | custom-call | flops 32212254720 | bytes 31457280 | tf_op jit(solution)/shard_map/combine/pallas_call | solution.py:833
  167.5 2.0 collective-permute-done.4
  169.5 1.3 fusion
  170.8 49.9 %shared_gradients.1 = (bf16[16,512,128]{2,1,0:T(8,128)(2,1)}, f32[16,512]{1,0:T(8,128)}, f32[1024,512]{1,0:T(8,128)}) custom-call(s32[1,1024]{1,0:T(1,128)} %bitcast.22, f32[8,4,256]{2,1,0:T(4,128)} %get-tuple-element.51.lse, f32[16,512]{1,0:T(8,128)} %get-tuple-element.64.partial, f32[1,512]{1,0:T(1,128)} %bitcast.18, ...), custom_call_target="tpu_custom_call" | custom-call | flops 3221225472 | bytes 16777216 | tf_op jit(solution)/shard_map/shared_gradients/pallas_call | solution.py:1268
  220.8 1.6 copy-done.1
  222.4 1.6 copy-done.2
  224.0 0.8 copy-done.6
  224.7 4.2 %finish.1 = (f32[512,1536]{1,0:T(8,128)}, f32[512,512]{1,0:T(8,128)}, f32[1,512,512]{2,1,0:T(8,128)}, f32[1,512,512]{2,1,0:T(8,128)}, f32[8,512]{1,0:T(8,128)S(1...) custom-call(bf16[16,512,128]{2,1,0:T(8,128)(2,1)S(1)} %copy-done.1, bf16[1024,512]{1,0:T(8,128)(2,1)S(1)} %collective-permute-done.5.ring, ...), custom_call_target="tpu_custom_call" | custom-call | bytes 14680064 | tf_op jit(solution)/shard_map/finish/pallas_call | solution.py:1343
  230.1 0.7 copy.32
  (44 shorter events, 3.5 us)
Async XLA Ops:
  0.6 31.1 %collective-permute-start = (bf16[512,512]{1,0:T(8,128)(2,1)}, bf16[512,512]{1,0:T(8,128)(2,1)S(1)}, u32[]{:S(2)}, u32[]{:S(2)}) collective-permute-start(bf16[512,512]{1,0:T(8,128)(2,1)} %bitcast.25), channel_id=1, source_target_pairs={{0,1},{1,2},{2,3},{3,0},{4,5},{5,6},{6,7},{7,4},{8,9},{9,10},{10,1... | collective-permute-start | bytes 1572872 | tf_op jit(solution)/shard_map/ppermute | solution.py:1397
  3.7 28.0 %collective-permute-start.1 = (bf16[512,512]{1,0:T(8,128)(2,1)}, bf16[512,512]{1,0:T(8,128)(2,1)}, u32[]{:S(2)}, u32[]{:S(2)}) collective-permute-start(bf16[512,512]{1,0:T(8,128)(2,1)} %bitcast.27), channel_id=1, source_target_pairs={{0,1},{1,2},{2,3},{3,0},{4,5},{5,6},{6,7},{7,4},{8,9},{9,10},{10,1... | collective-permute-start | bytes 1572872 | tf_op jit(solution)/shard_map/ppermute | solution.py:1397
  6.2 1.4 copy-start.3
  7.6 1.2 copy-start.4
  8.9 0.7 copy-start.7
  9.5 1.2 copy-start.8
  10.8 0.7 copy-start.9
  20.0 1.7 copy-start
  21.7 1.0 copy-start.5
  22.7 0.8 copy-start.10
  23.5 0.6 copy-start.11
  24.1 0.6 copy-start.12
  24.7 3.9 %copy-start.15 = (s32[1024]{0:T(1024)S(1)}, s32[1024]{0:T(1024)}, u32[]{:S(2)}) copy-start(s32[1024]{0:T(1024)} %param.15) | copy-start | bytes 12292
  24.7 4.1 %copy-start.16 = (bf16[512,8]{0,1:T(8,128)(2,1)S(1)}, bf16[512,8]{0,1:T(8,128)(2,1)}, u32[]{:S(2)}) copy-start(bf16[512,8]{0,1:T(8,128)(2,1)} %param.22) | copy-start | bytes 24580
  24.7 5.1 %copy-start.17 = (s32[8]{0:T(128)S(1)}, s32[8]{0:T(128)}, u32[]{:S(2)}) copy-start(s32[8]{0:T(128)} %constant.30.clone) | copy-start | bytes 100
  24.7 5.1 %copy-start.18 = (s32[8]{0:T(128)S(1)}, s32[8]{0:T(128)}, u32[]{:S(2)}) copy-start(s32[8]{0:T(128)} %constant.29.clone) | copy-start | bytes 100
  24.7 34.5 %all-to-all-start = ((bf16[8,272,512]{2,1,0:T(8,128)(2,1)}), bf16[8,272,512]{2,1,0:T(8,128)(2,1)S(1)}, u32[]{:S(2)}, u32[]{:S(2)}) async-start(bf16[8,272,512]{2,1,0:T(8,128)(2,1)} %get-tuple-element.57), calls=%async_computation | async-start | bytes 4456448 | tf_op jit(solution)/shard_map/all_to_all | solution.py:1404
  31.7 18.8 %copy-start.19 = (bf16[512,512]{1,0:T(8,128)(2,1)}, bf16[512,512]{1,0:T(8,128)(2,1)S(1)}, u32[]{:S(2)}) copy-start(bf16[512,512]{1,0:T(8,128)(2,1)S(1)} %collective-permute-done.w_in1) | copy-start | bytes 1572868
  31.7 18.8 %collective-permute-start.2 = (bf16[512,512]{1,0:T(8,128)(2,1)S(1)}, bf16[512,512]{1,0:T(8,128)(2,1)S(1)}, u32[]{:S(2)}, u32[]{:S(2)}) collective-permute-start(bf16[512,512]{1,0:T(8,128)(2,1)S(1)} %collective-permute-done.w_in1), channel_id=1, source_target_pairs={{0,1},{1,2},{2,3},{3,0},{4,5},{5,6},{6,7},{7,4},{8,9},{9,10},{10,1... | collective-permute-start | bytes 1572872 | tf_op jit(solution)/shard_map/ppermute | solution.py:1397
  33.4 25.9 %collective-permute-start.3 = (bf16[512,512]{1,0:T(8,128)(2,1)}, bf16[512,512]{1,0:T(8,128)(2,1)}, u32[]{:S(2)}, u32[]{:S(2)}) collective-permute-start(bf16[512,512]{1,0:T(8,128)(2,1)} %collective-permute-done.1.w_out1), channel_id=1, source_target_pairs={{0,1},{1,2},{2,3},{3,0},{4,5},{5,6},{6,7},{7,4},{8,9},{9,10},{10,1... | collective-permute-start | bytes 1572872 | tf_op jit(solution)/shard_map/ppermute | solution.py:1397
  50.6 0.8 copy-start.20
  59.3 1.4 copy-start.13
  142.3 27.2 %collective-permute-start.4 = (bf16[1024,512]{1,0:T(8,128)(2,1)}, bf16[1024,512]{1,0:T(8,128)(2,1)S(1)}, u32[]{:S(2)}, u32[]{:S(2)}) collective-permute-start(bf16[1024,512]{1,0:T(8,128)(2,1)} %get-tuple-element.66), channel_id=1, source_target_pairs={{0,1},{1,2},{2,3},{3,0},{4,5},{5,6},{6,7},{7,4},{8,9},{9,10},{10,1... | collective-permute-start | bytes 3145736 | tf_op jit(solution)/shard_map/ppermute | solution.py:1397
  143.8 25.7 %copy-start.14 = (bf16[2,1024,512]{2,1,0:T(8,128)(2,1)S(1)}, bf16[2,1024,512]{2,1,0:T(8,128)(2,1)}, u32[]{:S(2)}) copy-start(bf16[2,1024,512]{2,1,0:T(8,128)(2,1)} %get-tuple-element.75) | copy-start | bytes 6291460
  170.8 50.0 %collective-permute-start.5 = (bf16[1024,512]{1,0:T(8,128)(2,1)}, bf16[1024,512]{1,0:T(8,128)(2,1)S(1)}, u32[]{:S(2)}, u32[]{:S(2)}) collective-permute-start(bf16[1024,512]{1,0:T(8,128)(2,1)} %fusion), channel_id=1, source_target_pairs={{0,1},{1,2},{2,3},{3,0},{4,5},{5,6},{6,7},{7,4},{8,9},{9,10},{10,1... | collective-permute-start | bytes 3145736 | tf_op jit(solution)/shard_map/ppermute | solution.py:1397
  220.8 1.6 copy-start.1
  222.4 1.6 copy-start.2
  224.0 0.8 copy-start.6
